TPU v7x, 32 devices: a whole 2x2x4 slice. The times are simulated.
32 devices in a mesh: req: 32 (over z, y, x, core), mlp: 1.
Axes of the slice: x: 2, y: 2, z: 4, core: 2. Of those that a mesh axis runs over, the one named last changes fastest.
Arguments:
- tokens: bfloat16 [12288, 2048], P(('req', 'mlp')), may hold values from -6 to 6
- lengths: int32 [4], replicated, may hold values from 1 to 6144, 12288 in all
- in_gain: float32 [2048], replicated, may hold values from 0.5 to 1.5
- w_query: bfloat16 [2048, 2048], P(None, 'mlp'), may hold values from -0.125 to 0.125
- w_key: bfloat16 [2048, 2048], P(None, 'mlp'), may hold values from -1 to 1
- w_value: bfloat16 [2048, 4096], P(None, 'mlp'), may hold values from -0.125 to 0.125
- w_gate: bfloat16 [2048, 4096], P(None, 'mlp'), may hold values from -0.125 to 0.125
- w_beta: bfloat16 [2048, 16], P(None, 'mlp'), may hold values from -0.125 to 0.125
- w_decay: bfloat16 [2048, 16], P(None, 'mlp'), may hold values from -0.125 to 0.125
- decay_log: float32 [16], P('mlp'), may hold values from -11 to 0
- decay_bias: float32 [16], P('mlp'), may hold values from -3 to 1
- conv_query: float32 [4, 2048], P(None, 'mlp'), may hold values from -2.5 to 2.5
- conv_key: float32 [4, 2048], P(None, 'mlp'), may hold values from -2.5 to 2.5
- conv_value: float32 [4, 4096], P(None, 'mlp'), may hold values from -2.5 to 2.5
- head_gain: float32 [256], replicated, may hold values from 0.5 to 1.5
- w_out: bfloat16 [4096, 2048], P('mlp'), may hold values from -0.09375 to 0.09375
- mlp_gain: float32 [2048], replicated, may hold values from 0.5 to 1.5
- w_up_gate: bfloat16 [2048, 5632], P('req', 'mlp'), may hold values from -0.125 to 0.125
- w_up: bfloat16 [2048, 5632], P('req', 'mlp'), may hold values from -0.125 to 0.125
- w_down: bfloat16 [5632, 2048], P('mlp', 'req'), may hold values from -0.078125 to 0.078125
Outputs:
- layer_out: bfloat16 [12288, 2048], P(('req', 'mlp'))
Inputs may be any that keep to these rules, and one draw needn't show every extreme that they name: The 4 prompts lie end to end in the order given and their lengths sum to 12288; the longest has exactly 6144 tokens.
All inputs are finite; a program needn't handle non-finite values.
Results may differ from a plain program's by a relative error of at most 0.017.
Values may be sent and summed in bfloat16 or wider, within the bound.
A program may use at most 384 MiB of HBM per device.

v0:
```python
import jax
import jax.numpy as jnp
from jax import lax
from jax.sharding import PartitionSpec as P

GROUP = 64


maximal_matmul_accuracy = lax.Precision.HIGHEST


def shifted(value, axis, steps):
    count = lax.axis_size(axis)
    first, last = (max(0, -steps), min(count, count - steps))
    return lax.ppermute(value, axis, [(source, source + steps) for source in range(first, last)])


def carried_in(shard, axis, combine, identity):
    length, index = (lax.axis_size(axis), lax.axis_index(axis))
    everything = jax.tree.map(
        lambda part, kind: lax.all_gather(part.astype(kind), axis),
        shard,
        jax.tree.map(lambda a: jnp.bfloat16 if a.dtype == jnp.float32 else a.dtype, shard),
    )
    start = jax.tree.map(
        lambda part, zero: jnp.broadcast_to(jnp.asarray(zero, part.dtype), part.shape),
        shard,
        identity,
    )

    def step(k, before):
        reached = k < index
        new = combine(
            before, jax.tree.map(lambda part, own: part[k].astype(own.dtype), everything, shard)
        )
        return jax.tree.map(lambda a, b: jnp.where(reached, a, b), new, before)

    return lax.fori_loop(0, length, step, start)


def rms_scale(values, gain):
    mean_square = jnp.mean(values * values, axis=-1, keepdims=True)
    return values / jnp.sqrt(mean_square + 1e-06) * gain


def unit_norm(values):
    return values / jnp.sqrt(jnp.sum(values * values, axis=-1, keepdims=True) + 1e-06)


def segment_of(positions, lengths):
    bounds = jnp.cumsum(lengths)[:-1]
    return jnp.sum((positions[:, None] >= bounds[None, :]).astype(jnp.int32), axis=1)


def causal_conv(projected, rim_rows, kernel, segment_ids, rim_segments):
    taps_count = kernel.shape[0]
    row_count = projected.shape[0]
    extended = jnp.concatenate([rim_rows, projected], axis=0).astype(jnp.float32)
    extended_ids = jnp.concatenate([rim_segments, segment_ids], axis=0)
    accumulated = jnp.zeros(projected.shape, jnp.float32)
    for offset in range(taps_count):
        window = lax.slice_in_dim(extended, offset, offset + row_count, axis=0)
        window_ids = lax.slice_in_dim(extended_ids, offset, offset + row_count, axis=0)
        same_doc = (window_ids == segment_ids)[:, None]
        accumulated = accumulated + kernel[offset][None, :] * jnp.where(same_doc, window, 0.0)
    return accumulated


def group_parts(query_vecs, key_vecs, value_vecs, beta_vals, log_decay, segment_ids, prior_segment):
    group_rows = query_vecs.shape[0]
    value_dim = value_vecs.shape[-1]
    cumulative = jnp.cumsum(log_decay, axis=0)
    row_index = jnp.arange(group_rows)[:, None]
    col_index = jnp.arange(group_rows)[None, :]
    same_doc = segment_ids[:, None] == segment_ids[None, :]
    keep_mask = ((row_index >= col_index) & same_doc)[None, :, :]
    strict_mask = (row_index > col_index)[None, :, :]
    head_cumul = jnp.transpose(cumulative)
    gaps = head_cumul[:, :, None] - head_cumul[:, None, :]
    weights = jnp.where(keep_mask, jnp.exp(jnp.where(keep_mask, gaps, 0.0)), 0.0)
    open_mask = (segment_ids == prior_segment).astype(query_vecs.dtype)
    start_decay = jnp.exp(cumulative) * open_mask[:, None]
    key_dots = jnp.einsum("ihd,jhd->hij", key_vecs, key_vecs, precision=maximal_matmul_accuracy)
    coupling = jnp.where(
        strict_mask, jnp.transpose(beta_vals)[:, :, None] * weights * key_dots, 0.0
    )
    system = coupling + jnp.eye(group_rows, dtype=query_vecs.dtype)[None]
    targets = jnp.concatenate(
        [beta_vals[:, :, None] * value_vecs, (beta_vals * start_decay)[:, :, None] * key_vecs],
        axis=-1,
    )
    solved = jax.scipy.linalg.solve_triangular(
        system, jnp.transpose(targets, (1, 0, 2)), lower=True, unit_diagonal=True
    )
    starting_value_rows = solved[:, :, :value_dim]
    delta_correction = solved[:, :, value_dim:]
    query_dots = weights * jnp.einsum(
        "ihd,jhd->hij", query_vecs, key_vecs, precision=maximal_matmul_accuracy
    )
    query_begin_offset = query_vecs * start_decay[:, :, None]
    final_key_rows = key_vecs * jnp.transpose(weights[:, -1, :])[:, :, None]
    carried_decay_factor = start_decay[-1]
    return (
        starting_value_rows,
        delta_correction,
        query_dots,
        query_begin_offset,
        final_key_rows,
        carried_decay_factor,
    )


def group_step(running_state, parts):
    (
        starting_value_rows,
        delta_correction,
        query_dots,
        query_begin_offset,
        final_key_rows,
        carried_decay_factor,
    ) = parts
    fresh_state_update = starting_value_rows - jnp.einsum(
        "mxf,mft->mxt", delta_correction, running_state, precision=maximal_matmul_accuracy
    )
    output_rows = jnp.einsum(
        "fob,obt->fot", query_begin_offset, running_state, precision=maximal_matmul_accuracy
    )
    output_rows = output_rows + jnp.einsum(
        "hij,hjv->ihv", query_dots, fresh_state_update, precision=maximal_matmul_accuracy
    )
    updated_state = carried_decay_factor[:, None, None] * running_state + jnp.einsum(
        "new,enr->ewr", final_key_rows, fresh_state_update, precision=maximal_matmul_accuracy
    )
    return (updated_state, output_rows)


def combine_maps(earlier, later):
    earlier_map, preceding_additive = earlier
    following_linear_map, following_additive = later
    joined_map = jnp.einsum(
        "hkl,hlm->hkm", following_linear_map, earlier_map, precision=maximal_matmul_accuracy
    )
    joined_add = (
        jnp.einsum(
            "baf,bfu->bau",
            following_linear_map,
            preceding_additive,
            precision=maximal_matmul_accuracy,
        )
        + following_additive
    )
    return (joined_map, joined_add)


def per_device(
    tokens,
    lengths,
    in_gain,
    w_query,
    w_key,
    w_value,
    w_gate,
    w_beta,
    w_decay,
    decay_log,
    decay_bias,
    conv_query,
    conv_key,
    conv_value,
    head_gain,
    w_out,
    mlp_gain,
    w_up_gate,
    w_up,
    w_down,
):
    share_rows = tokens.shape[0]
    gathered = lax.all_gather(tokens, "mlp", axis=0, tiled=True)
    piece_len = gathered.shape[0]
    head_count = w_beta.shape[1]
    key_dim = w_query.shape[1] // head_count
    value_dim = w_value.shape[1] // head_count
    taps_count = conv_query.shape[0]
    group_count = piece_len // GROUP
    piece_start = lax.axis_index("req") * piece_len
    positions = piece_start + jnp.arange(piece_len, dtype=jnp.int32)
    segment_ids = segment_of(positions, lengths)
    rim_segments = segment_of(
        piece_start - (taps_count - 1) + jnp.arange(taps_count - 1, dtype=jnp.int32), lengths
    )
    token_rows = gathered.astype(jnp.float32)
    normed = rms_scale(token_rows, in_gain).astype(jnp.bfloat16)
    proj_query = jnp.dot(normed, w_query, preferred_element_type=jnp.float32).astype(jnp.bfloat16)
    proj_key = jnp.dot(normed, w_key, preferred_element_type=jnp.float32).astype(jnp.bfloat16)
    proj_value = jnp.dot(normed, w_value, preferred_element_type=jnp.float32).astype(jnp.bfloat16)
    edge_rows = jnp.concatenate(
        [
            proj_query[piece_len - taps_count + 1 :],
            proj_key[piece_len - taps_count + 1 :],
            proj_value[piece_len - taps_count + 1 :],
        ],
        axis=1,
    )
    rim_all = shifted(edge_rows, "req", 1)
    query_width = proj_query.shape[1]
    key_width = proj_key.shape[1]
    rim_query = rim_all[:, :query_width]
    rim_key = rim_all[:, query_width : query_width + key_width]
    rim_value = rim_all[:, query_width + key_width :]
    conv_q = jax.nn.silu(causal_conv(proj_query, rim_query, conv_query, segment_ids, rim_segments))
    conv_k = jax.nn.silu(causal_conv(proj_key, rim_key, conv_key, segment_ids, rim_segments))
    conv_v = jax.nn.silu(causal_conv(proj_value, rim_value, conv_value, segment_ids, rim_segments))
    query_vecs = unit_norm(conv_q.reshape(piece_len, head_count, key_dim)) * key_dim ** (-0.5)
    key_vecs = unit_norm(conv_k.reshape(piece_len, head_count, key_dim))
    value_vecs = conv_v.reshape(piece_len, head_count, value_dim)
    gate_lin = jnp.dot(normed, w_gate, preferred_element_type=jnp.float32).astype(jnp.bfloat16)
    beta_vals = jax.nn.sigmoid(jnp.dot(normed, w_beta, preferred_element_type=jnp.float32))
    log_decay = -jnp.exp(decay_log) * jax.nn.softplus(
        jnp.dot(normed, w_decay, preferred_element_type=jnp.float32) + decay_bias
    )

    def shaped(values):
        return values.reshape((group_count, GROUP) + values.shape[1:])

    prior_ids = segment_of(
        piece_start + jnp.arange(group_count, dtype=jnp.int32) * GROUP - 1, lengths
    )
    parts = jax.vmap(group_parts)(
        shaped(query_vecs),
        shaped(key_vecs),
        shaped(value_vecs),
        shaped(beta_vals),
        shaped(log_decay),
        shaped(segment_ids),
        prior_ids,
    )
    eye_block = jnp.broadcast_to(
        jnp.eye(key_dim, dtype=jnp.float32), (head_count, key_dim, key_dim)
    )
    zero_state = jnp.zeros((head_count, key_dim, value_dim), jnp.float32)

    def compose(carried, parts_one):
        (
            starting_value_rows,
            delta_correction,
            query_dots,
            query_begin_offset,
            final_key_rows,
            carried_decay_factor,
        ) = parts_one
        local_map = carried_decay_factor[:, None, None] * eye_block - jnp.einsum(
            "chk,hcl->hkl", final_key_rows, delta_correction, precision=maximal_matmul_accuracy
        )
        within_piece_additive = jnp.einsum(
            "new,enr->ewr", final_key_rows, starting_value_rows, precision=maximal_matmul_accuracy
        )
        return (combine_maps(carried, (local_map, within_piece_additive)), None)

    piece_maps, _ = lax.scan(compose, (eye_block, zero_state), parts)
    incoming = carried_in(piece_maps, "req", combine_maps, (eye_block, zero_state))
    _, output_rows = lax.scan(group_step, incoming[1], parts)
    output_rows = output_rows.reshape(piece_len, head_count, value_dim)
    gate_vals = jax.nn.silu(gate_lin.astype(jnp.float32)).reshape(piece_len, head_count, value_dim)
    head_out = (
        (rms_scale(output_rows, head_gain) * gate_vals)
        .reshape(piece_len, head_count * value_dim)
        .astype(jnp.bfloat16)
    )
    partial_out = jnp.dot(head_out, w_out, preferred_element_type=jnp.float32)
    attn_sum = lax.psum(partial_out.astype(jnp.bfloat16), "mlp").astype(jnp.float32)
    resid = token_rows + attn_sum
    mlp_in = rms_scale(resid, mlp_gain).astype(jnp.bfloat16)
    resid_mine = lax.dynamic_slice_in_dim(resid, lax.axis_index("mlp") * share_rows, share_rows, 0)

    def add_rows(piece):
        return jnp.dot(mlp_in, piece, preferred_element_type=jnp.float32)

    gate_acc = add_rows(lax.all_gather(w_up_gate, "req", axis=0, tiled=True))
    up_acc = add_rows(lax.all_gather(w_up, "req", axis=0, tiled=True))
    hidden = (jax.nn.silu(gate_acc) * up_acc).astype(jnp.bfloat16)
    down_terms = jnp.dot(
        hidden,
        lax.all_gather(w_down, "req", axis=1, tiled=True),
        preferred_element_type=jnp.float32,
    )
    mlp_share = lax.psum_scatter(
        down_terms.astype(jnp.bfloat16), "mlp", scatter_dimension=0, tiled=True
    ).astype(jnp.float32)
    return (resid_mine + mlp_share).astype(jnp.bfloat16)


def solution(mesh):
    placed = (
        P(("req", "mlp"), None),
        P(),
        P(),
        P(None, "mlp"),
        P(None, "mlp"),
        P(None, "mlp"),
        P(None, "mlp"),
        P(None, "mlp"),
        P(None, "mlp"),
        P("mlp"),
        P("mlp"),
        P(None, "mlp"),
        P(None, "mlp"),
        P(None, "mlp"),
        P(),
        P("mlp", None),
        P(),
        P("req", "mlp"),
        P("req", "mlp"),
        P("mlp", "req"),
    )
    return jax.shard_map(
        per_device, mesh=mesh, in_specs=placed, out_specs=P(("req", "mlp"), None), check_vma=False
    )
```

profile of v0, /device:TPU:0, one launch (start us, length us, event | category | flops | bytes accessed | tf_op | source)
XLA Modules:
  0.0 1460.8 jit_solution(11597744085855988638)
XLA Ops:
  10.5 11.6 convolution_convert_fusion.1
  22.2 3.5 convolution_convert_fusion.4
  25.8 3.5 convolution_convert_fusion.3
  52.3 6.5 multiply_bitcast_fusion
  66.6 8.5 add_bitcast_fusion
  75.0 472.5 %custom-call.4 = f32[6,16,1,64,64]{3,4,2,1,0:T(8,128)S(1)} custom-call(f32[6,16,1,64,64]{4,3,2,1,0:T(8,128)} %add_bitcast_fusion), custom_call_target="InvertDiagBlocksLowerTriangular" | custom-call | tf_op jit(solution)/shard_map/vmap(jit(_solve_triangular))/vmap()/triangular_solve | solution.py:92
  551.2 5.3 divide_multiply_fusion
  559.4 5.3 broadcast_multiply_fusion.1
  564.7 3.7 copy_multiply_fusion
  568.4 10.8 fusion.49
  585.5 84.5 %while.40 = (s32[]{:T(128)}, f32[16,128,128]{2,1,0:T(8,128)}, f32[16,128,256]{2,1,0:T(8,128)}, f32[6,16]{1,0:T(8,128)}, f32[6,64,16,128]{3,1,2,0:T(8,128)}, /*in...) while((s32[]{:T(128)}, f32[16,128,128]{2,1,0:T(8,128)}, ...), condition=%wide.region_8.9_spmd.clone, body=%wide.region_7.8_spmd.clone.sunk | while | flops 1813512192 | bytes 26806604 | solution.py:259
  675.7 4.2 copy.132
  685.6 3.5 broadcast_multiply_fusion
  689.1 8.2 fusion.87
  697.3 92.0 %all-gather.14.cloned.1.call-done = bf16[512,128,128]{2,1,0:T(8,128)(2,1)} async-done(((bf16[16,128,128]{2,1,0:T(8,128)(2,1)}), bf16[512,128,128]{2,1,0:T(8,128)(2,1)}) %all-gather.14.cloned.1.call-update) | async-done | bytes 16777232 | tf_op jit(solution)/shard_map/all_gather | solution.py:21
  789.4 195.8 %all-gather.16.cloned.1.call-done = bf16[512,128,256]{2,1,0:T(8,128)(2,1)} async-done(((bf16[16,128,256]{2,1,0:T(8,128)(2,1)}), bf16[512,128,256]{2,1,0:T(8,128)(2,1)}) %all-gather.16.cloned.1.call-update) | async-done | bytes 33554448 | tf_op jit(solution)/shard_map/all_gather | solution.py:21
  985.2 105.0 %while.41 = (s32[]{:T(128)}, f32[16,128,256]{2,1,0:T(8,128)S(1)}, s32[]{:T(128)}, bf16[32,16,128,128]{3,2,1,0:T(8,128)(2,1)}, bf16[32,16,128,256]{3,2,1,0:T(8,128)(2,1)}, /*index=5*/s32[]{:T(128)}, s32[]{:T(128)}) while((s32[]{:T(128)}, f32[16,128,256]{2,1,0:T(8,128)S(1)}, s32[]{:T(128)}, bf16[32,16,128,128]{3,2,1,0:T(8,128)(2,1)}, ...), condition=%wide.region_10.11_spmd.clone, body=%wide.region_9.10_spmd.clone.sunk | while | flops 807927808 | bytes 12061279 | solution.py:38
  1090.2 75.2 %while.39 = (s32[]{:T(128)}, f32[16,128,256]{2,1,0:T(8,128)S(1)}, f32[6,64,16,256]{3,1,2,0:T(8,128)}, f32[6,16]{1,0:T(8,128)}, f32[6,64,16,128]{3,1,2,0:T(8,128)...) while((s32[]{:T(128)}, f32[16,128,256]{2,1,0:T(8,128)S(1)}, ...), condition=%wide.region_13.14_spmd, body=%wide.region_12.13_spmd.sunk | while | flops 1410859008 | bytes 17829160 | solution.py:261
  1099.2 3.5 multiply_add_fusion.2
  1111.6 3.5 multiply_add_fusion.2
  1124.1 3.5 multiply_add_fusion.2
  1136.5 3.5 multiply_add_fusion.2
  1149.1 3.5 multiply_add_fusion.2
  1161.5 3.5 multiply_add_fusion.2
  1165.5 9.2 copy.120
  1176.6 8.7 copy.134
  1185.3 8.9 copy.133
  1194.2 24.5 %multiply_reduce_fusion.1 = (f32[384]{0:T(512)S(1)}, bf16[384,2048]{1,0:T(8,128)(2,1)}) fusion(bf16[384,2048]{1,0:T(8,128)(2,1)S(1)} %copy-done.10, bf16[4096,2048]{1,0:T(8,128)(2,1)} %param.41, f32[384,4096]{1,0:T(8,128)} %bitcast.206, f32[384,4096]{1,0:T(8,128)} %bitcast.205, f32[4096]{0:T(1024)S(1)} %bitcast.226, bf16[384,2048]{1,0:T(8,128)(2,1)S(1)} %copy-done.6, ...), kind=kOutput, calls=%fused_computation.112 | convolution fusion | flops 12905349120 | bytes 50873856 | tf_op jit(solution)/shard_map/dot_general | solution.py:269
  1218.7 16.7 %fusion.102 = f32[384,5632]{1,0:T(8,128)} fusion(bf16[2048,5632]{1,0:T(8,128)(2,1)} %all-gather.8.cloned.1.call-done, bf16[384,2048]{1,0:T(8,128)(2,1)} %get-tuple-element.313, bf16[384,2048]{1,0:T(8,128)(2,1)S(1)} %copy-done.10, f32[2048]{0:T(1024)S(1)} %copy-done.48, f32[384]{0:T(512)S(1)} %add_sqrt_fusion.3), kind=kOutput, calls=%fused_computation.178 | convolution fusion | flops 8863088640 | bytes 34874880 | tf_op jit(solution)/shard_map/dot_general | solution.py:276
  1235.4 41.0 %all-gather.10.cloned.1.call-done = bf16[2048,5632]{1,0:T(8,128)(2,1)} async-done(((bf16[64,5632]{1,0:T(8,128)(2,1)}), bf16[2048,5632]{1,0:T(8,128)(2,1)}) %all-gather.10.cloned.1.call-update) | async-done | bytes 23068688 | tf_op jit(solution)/shard_map/all_gather | solution.py:279
  1276.4 145.5 %all-gather.12.cloned.1.call-done = bf16[5632,2048]{0,1:T(8,128)(2,1)} async-done(((bf16[5632,64]{0,1:T(8,128)(2,1)}), bf16[5632,2048]{0,1:T(8,128)(2,1)}) %all-gather.12.cloned.1.call-update) | async-done | bytes 23068688 | tf_op jit(solution)/shard_map/all_gather | solution.py:283
  1421.9 32.2 %add_convert_fusion = bf16[384,2048]{1,0:T(8,128)(2,1)} fusion(bf16[384,2048]{1,0:T(8,128)(2,1)} %get-tuple-element.313, bf16[384,2048]{1,0:T(8,128)(2,1)S(1)} %copy-done.10, bf16[5632,2048]{0,1:T(8,128)(2,1)} %all-gather.12.cloned.1.call-done, bf16[2048,5632]{1,0:T(8,128)(2,1)} %all-gather.10.cloned.1.call-done, f32[384,5632]{1,0:T(8,128)} %fusion.102, ...), kind=kOutput, calls=%fused_computation.110 | convolution fusion | flops 17739939840 | bytes 59516416 | tf_op jit(solution)/shard_map/dot_general | solution.py:281
  (349 shorter events, 301.9 us)
Async XLA Ops:
  6.5 31.0 %copy-start = (bf16[2048,16]{0,1:T(8,128)(2,1)S(1)}, bf16[2048,16]{0,1:T(8,128)(2,1)}, u32[]{:S(2)}) copy-start(bf16[2048,16]{0,1:T(8,128)(2,1)} %param.34) | copy-start | bytes 196612
  6.5 782.8 %all-gather.14.cloned.1.call-start = ((), (), s32[]{:S(2)}) async-start(), calls=%async_computation.3 | async-start | bytes 17301504 | tf_op jit(solution)/shard_map/all_gather | solution.py:21
  8.4 13.8 slice-start.2
  8.4 17.4 %slice-start.4 = ((s8[8388608]{0:T(1024)(128)(4,1)}), s8[4194304]{0:T(1024)(128)(4,1)S(1)}, s32[]{:S(2)}) async-start(s8[8388608]{0:T(1024)(128)(4,1)} %bitcast.230), calls=%async_computation.9 | async-start | bytes 8388608
  10.5 28.0 %copy-start.5 = (bf16[384,2048]{1,0:T(8,128)(2,1)}, bf16[384,2048]{1,0:T(8,128)(2,1)S(1)}, u32[]{:S(2)}) copy-start(bf16[384,2048]{1,0:T(8,128)(2,1)S(1)} %fusion.66) | copy-start | bytes 4718596
  10.5 11.6 slice-start.3
  10.5 15.2 %slice-start.5 = ((s8[8388608]{0:T(1024)(128)(4,1)}), s8[4194304]{0:T(1024)(128)(4,1)S(1)}, s32[]{:S(2)}) async-start(s8[8388608]{0:T(1024)(128)(4,1)} %bitcast.230), calls=%async_computation.10 | async-start | bytes 8388608
  22.1 3.6 copy-start.11
  25.7 3.7 copy-start.12
  25.8 9.2 copy-start.49
  25.8 10.5 copy-start.34
  25.8 11.1 copy-start.35
  25.8 11.7 copy-start.50
  25.8 11.7 copy-start.47
  25.8 12.7 copy-start.24
  29.4 11.5 copy-start.25
  31.2 17.3 %collective-permute-start = (bf16[3,8192]{1,0:T(4,128)(2,1)}, bf16[3,8192]{1,0:T(4,128)(2,1)}, u32[]{:S(2)}, u32[]{:S(2)}) collective-permute-start(bf16[3,8192]{1,0:T(4,128)(2,1)} %pad_maximum_fusion), channel_id=1, source_target_pairs={{0,1},{1,2},{2,3},{3,4},{4,5},{5,6},{6,7},{7,8},{8,9},{9,10},{10,1... | collective-permute-start | bytes 147464 | tf_op jit(solution)/shard_map/ppermute | solution.py:15
  559.4 5.3 copy-start.15
  650.5 3.3 copy-start.3
  672.4 312.8 %all-gather.16.cloned.1.call-start = ((), (), s32[]{:S(2)}) async-start(), calls=%async_computation.4 | async-start | bytes 34603008 | tf_op jit(solution)/shard_map/all_gather | solution.py:21
  673.6 545.1 %all-gather.8.cloned.1.call-start = ((), (), s32[]{:S(2)}) async-start(), calls=%async_computation | async-start | bytes 23789568 | tf_op jit(solution)/shard_map/all_gather | solution.py:278
  674.3 602.1 %all-gather.10.cloned.1.call-start = ((), (), s32[]{:S(2)}) async-start(), calls=%async_computation.1 | async-start | bytes 23789568 | tf_op jit(solution)/shard_map/all_gather | solution.py:279
  674.9 747.0 %all-gather.12.cloned.1.call-start = ((), (), s32[]{:S(2)}) async-start(), calls=%async_computation.2 | async-start | bytes 23789568 | tf_op jit(solution)/shard_map/all_gather | solution.py:283
  685.5 3.6 copy-start.9
  685.6 3.5 copy-start.19
  1165.5 9.2 copy-start.4
  1175.7 9.6 slice-start
  1176.6 8.7 slice-start.1
  1185.3 8.9 copy-start.6
  1185.3 8.9 copy-start.10
  1194.2 24.5 %copy-start.48 = (f32[2048]{0:T(1024)S(1)}, f32[2048]{0:T(1024)}, u32[]{:S(2)}) copy-start(f32[2048]{0:T(1024)} %param.42) | copy-start | bytes 24580
  1421.9 32.2 %copy-start.1 = (bf16[2048,16]{0,1:T(8,128)(2,1)S(1)}, bf16[2048,16]{0,1:T(8,128)(2,1)}, u32[]{:S(2)}) copy-start(bf16[2048,16]{0,1:T(8,128)(2,1)} %param.34) | copy-start | bytes 196612
  (36 other events, 99.6 us)
Sparse Core Ops, SparseCore 0:
  672.5 116.8 all-gather.13
  792.2 192.9 all-gather.15
  988.1 142.7 all-gather.7
  1133.6 142.7 all-gather.9
  1279.1 142.7 all-gather.11
where the time goes:
time: 1470 us; the launch traced here: 1460 us
  other arithmetic  523 us (36%)
  waiting for transfers between devices  476 us (32%)
  matrix products  359 us (24%)
  local copies, waits for them, and re-layouts  82.9 us (6%)
    another operation x2, other arithmetic, group_parts(): jax.scipy.linalg.solve_triangular(system, jnp.transpose(targets, (1, 0, 2...  472 us
    all_gather x2, waiting for transfers between devices, carried_in(): lax.all_gather(part.astype(kind), axis)  288 us
    all_gather x1, waiting for transfers between devices, per_device(): lax.all_gather(w_down, 'req', axis=1, tiled=True)  145 us
    dot_general x38, matrix products, combine_maps(): jnp.einsum('baf,bfu->bau', following_linear_map, preceding_additive, prec...  117 us
    all_gather x1, waiting for transfers between devices, per_device(): up_acc = add_rows(lax.all_gather(w_up, 'req', axis=0, tiled=True))  41 us
    unnamed x122, local copies, waits for them, and re-layouts  33.9 us
    dot_general x1, matrix products, per_device(): jnp.dot(hidden, lax.all_gather(w_down, 'req', axis=1, tiled=True), prefer...  32.2 us
  transfers between devices with their start and end apart: 6, of which 4 were waited for; matrix products, arithmetic and copies ran while one was open for 20% of the time, Pallas kernels for 0%

commit v1 on v0

v1 whole, which is shorter than its diff:
```python
import functools
import jax
import jax.numpy as jnp
from jax import lax
from jax.experimental import pallas as pl
from jax.experimental.pallas import tpu as pltpu
from jax.sharding import PartitionSpec as P

RIM = 16
F32 = jnp.float32
BF16 = jnp.bfloat16


def rms_scale(values, gain):
    mean_square = jnp.mean(values * values, axis=-1, keepdims=True)
    return values / jnp.sqrt(mean_square + 1e-06) * gain


def segment_of(positions, lengths):
    bounds = jnp.cumsum(lengths)[:-1]
    return jnp.sum((positions[:, None] >= bounds[None, :]).astype(jnp.int32), axis=1)


def mm(a, b):
    return jnp.dot(a, b, preferred_element_type=F32)


def mm_t(a, b):
    return lax.dot_general(a, b, (((1,), (1,)), ((), ())), preferred_element_type=F32)


def split(a):
    high = a.astype(BF16)
    return high, (a - high.astype(F32)).astype(BF16)


def mm3(a, b):
    ah, al = a
    bh, bl = b
    return mm(ah, bh) + (mm(ah, bl) + mm(al, bh))


def conv_silu(p_ref, taps_ref, lanes, scratch, masks, rows):
    scratch[...] = p_ref[:, lanes].astype(F32)
    taps = taps_ref.shape[0]
    acc = None
    for i in range(taps):
        back = taps - 1 - i
        window = scratch[pl.ds(RIM - back, rows), :]
        term = taps_ref[i : i + 1, lanes] * window
        if back:
            term = term * masks[back - 1]
        acc = term if acc is None else acc + term
    return acc / (1.0 + jnp.exp(-acc))


def local_kernel(
    chunk, dk, dv, pq, pk, pv, tq, tk, tv, scal, qeff, oloc, maps, scr_q, scr_k, scr_v
):
    heads = scal.shape[0]
    rows = scal.shape[2]
    count = rows // chunk
    row_i = lax.broadcasted_iota(jnp.int32, (chunk, chunk), 0)
    col_i = lax.broadcasted_iota(jnp.int32, (chunk, chunk), 1)
    eye = (row_i == col_i).astype(F32)
    pairs = [(h, c) for h in range(heads) for c in range(count)]
    cols, lanes, keys, queries, values = [], [], [], [], []
    for h in range(heads):
        lane = scal[h]
        col = lane.T
        masks = [col[:, 6 + s : 7 + s] for s in range(3)]
        q = conv_silu(pq, tq, slice(h * dk, (h + 1) * dk), scr_q.at[h], masks, rows)
        k = conv_silu(pk, tk, slice(h * dk, (h + 1) * dk), scr_k.at[h], masks, rows)
        v = conv_silu(pv, tv, slice(h * dv, (h + 1) * dv), scr_v.at[h], masks, rows)
        q = q * (lax.rsqrt(jnp.sum(q * q, axis=-1, keepdims=True) + 1e-06) * dk ** (-0.5))
        k = k * lax.rsqrt(jnp.sum(k * k, axis=-1, keepdims=True) + 1e-06)
        cols.append(col)
        lanes.append(lane)
        queries.append(q.astype(BF16))
        keys.append(k.astype(BF16))
        values.append(v * col[:, 0:1])
    lower, attend, inverse = {}, {}, {}
    for h, c in pairs:
        part = slice(c * chunk, (c + 1) * chunk)
        col, lane = cols[h][part], lanes[h][:, part]
        kb, qb = keys[h][part], queries[h][part]
        keep = (row_i >= col_i) & (col[:, 5:6] == lane[5:6, :])
        gaps = col[:, 1:2] - lane[1:2, :]
        weights = jnp.where(keep, jnp.exp(jnp.where(keep, gaps, 0.0)), 0.0)
        dots = mm_t(jnp.concatenate([kb, qb], axis=0), kb)
        lower[h, c] = jnp.where(row_i > col_i, col[:, 0:1] * weights * dots[:chunk], 0.0)
        attend[h, c] = (weights * dots[chunk:]).astype(BF16)
    shift = 0
    while (1 << shift) < chunk:
        level = ((row_i >> shift) != (col_i >> shift)) & (
            (row_i >> (shift + 1)) == (col_i >> (shift + 1))
        )
        if shift == 0:
            for p in pairs:
                inverse[p] = eye - jnp.where(level, lower[p], 0.0)
        else:
            halves = {p: split(inverse[p]) for p in pairs}
            mid = {p: mm3(halves[p], split(jnp.where(level, lower[p], 0.0))) for p in pairs}
            for p in pairs:
                inverse[p] = inverse[p] - mm3(split(mid[p]), halves[p])
        shift += 1
    start = jnp.concatenate(
        [
            (
                lax.broadcasted_iota(jnp.int32, (dk, dk), 0)
                == lax.broadcasted_iota(jnp.int32, (dk, dk), 1)
            ).astype(F32),
            jnp.zeros((dk, dv), F32),
        ],
        axis=1,
    )
    state = [start for _ in range(heads)]
    for c in range(count):
        part = slice(c * chunk, (c + 1) * chunk)
        for h in range(heads):
            col, lane = cols[h][part], lanes[h][:, part]
            kb, qb = keys[h][part], queries[h][part]
            sd = col[:, 2:3]
            both = mm(jnp.concatenate([kb, qb], axis=0), state[h].astype(BF16))
            fresh = jnp.concatenate(
                [jnp.zeros((chunk, dk), F32), values[h][part]], axis=1
            ) - (col[:, 0:1] * sd) * both[:chunk]
            update = mm(inverse[h, c].astype(BF16), fresh.astype(BF16))
            out = sd * both[chunk:] + mm(attend[h, c], update.astype(BF16))
            qeff[h, part, :] = out[:, :dk].astype(BF16)
            oloc[h, part, :] = out[:, dk:].astype(BF16)
            final = (col[:, 3:4] * update).astype(BF16)
            state[h] = lane[4:5, 0:1] * state[h] + mm(kb.astype(F32).T.astype(BF16), final)
    for h in range(heads):
        maps[h] = state[h].astype(BF16)


def local_maps(pq, pk, pv, tq, tk, tv, scal, chunk, per_step):
    heads, extra, rows = scal.shape
    dk, dv = pq.shape[1] // heads, pv.shape[1] // heads
    ext = pq.shape[0]
    by_lane = lambda r, w: pl.BlockSpec((r, w * per_step), lambda g: (0, g))
    by_head = lambda r, w: pl.BlockSpec((per_step, r, w), lambda g: (g, 0, 0))
    taps = tq.shape[0]
    return pl.pallas_call(
        functools.partial(local_kernel, chunk, dk, dv),
        grid=(heads // per_step,),
        in_specs=[
            by_lane(ext, dk),
            by_lane(ext, dk),
            by_lane(ext, dv),
            by_lane(taps, dk),
            by_lane(taps, dk),
            by_lane(taps, dv),
            by_head(extra, rows),
        ],
        out_specs=[by_head(rows, dk), by_head(rows, dv), by_head(dk, dk + dv)],
        out_shape=[
            jax.ShapeDtypeStruct((heads, rows, dk), BF16),
            jax.ShapeDtypeStruct((heads, rows, dv), BF16),
            jax.ShapeDtypeStruct((heads, dk, dk + dv), BF16),
        ],
        scratch_shapes=[
            pltpu.VMEM((per_step, ext, dk), F32),
            pltpu.VMEM((per_step, ext, dk), F32),
            pltpu.VMEM((per_step, ext, dv), F32),
        ],
        compiler_params=pltpu.CompilerParams(vmem_limit_bytes=48 * 2**20),
        cost_estimate=pl.CostEstimate(
            flops=heads * rows * 2000000, bytes_accessed=20 * 2**20, transcendentals=0
        ),
        name="local_maps",
    )(pq, pk, pv, tq, tk, tv, scal)


def chain_kernel(n, dk, maps, states, landing, outgoing, send_sem, recv_sem):
    me = lax.axis_index("req")
    heads = maps.shape[0]
    barrier = pltpu.get_barrier_semaphore()
    has_left, has_right = me > 0, me < n - 1

    @pl.when(has_left)
    def _():
        pl.semaphore_signal(
            barrier, inc=1, device_id={"req": me - 1}, device_id_type=pl.DeviceIdType.MESH
        )

    @pl.when(has_right)
    def _():
        pl.semaphore_wait(barrier, 1)

    def copy(h):
        return pltpu.make_async_remote_copy(
            src_ref=outgoing.at[h],
            dst_ref=landing.at[h],
            send_sem=send_sem.at[h],
            recv_sem=recv_sem.at[h],
            device_id={"req": me + 1},
            device_id_type=pl.DeviceIdType.MESH,
        )

    def one(h, carry):
        @pl.when(has_left)
        def _():
            copy(h).wait_recv()
            coming = landing[h]
            states[h] = coming
            onward = mm(maps[h, :, :dk], coming) + maps[h, :, dk:].astype(F32)
            outgoing[h] = onward.astype(BF16)

        @pl.when(me == 0)
        def _():
            states[h] = jnp.zeros(states.shape[1:], BF16)
            outgoing[h] = maps[h, :, dk:]

        @pl.when(has_right)
        def _():
            copy(h).start()

        return carry

    lax.fori_loop(0, heads, one, 0)

    def drain(h, carry):
        copy(h).wait_send()
        return carry

    @pl.when(has_right)
    def _():
        lax.fori_loop(0, heads, drain, 0)


def chain_states(maps, n):
    heads, dk, width = maps.shape
    dv = width - dk
    return pl.pallas_call(
        functools.partial(chain_kernel, n, dk),
        in_specs=[pl.BlockSpec(memory_space=pltpu.VMEM)],
        out_specs=pl.BlockSpec(memory_space=pltpu.VMEM),
        out_shape=jax.ShapeDtypeStruct((heads, dk, dv), BF16),
        scratch_shapes=[
            pltpu.VMEM((heads, dk, dv), BF16),
            pltpu.VMEM((heads, dk, dv), BF16),
            pltpu.SemaphoreType.DMA((heads,)),
            pltpu.SemaphoreType.DMA((heads,)),
        ],
        compiler_params=pltpu.CompilerParams(
            collective_id=0, has_side_effects=True, vmem_limit_bytes=32 * 2**20
        ),
        cost_estimate=pl.CostEstimate(
            flops=60 * 10**9, bytes_accessed=3 * 2**20, transcendentals=0
        ),
        name="chain_states",
    )(maps)


def finish_kernel(qeff, oloc, states, gate, gain, out):
    heads, dv = oloc.shape[0], oloc.shape[2]
    for h in range(heads):
        lanes = slice(h * dv, (h + 1) * dv)
        rec = mm(qeff[h], states[h]) + oloc[h].astype(F32)
        rec = rec * lax.rsqrt(jnp.mean(rec * rec, axis=-1, keepdims=True) + 1e-06)
        g = gate[:, lanes].astype(F32)
        out[:, lanes] = (rec * gain[...] * (g / (1.0 + jnp.exp(-g)))).astype(BF16)


def finish_heads(qeff, oloc, states, gate, gain, per_step):
    heads, rows, dk = qeff.shape
    dv = oloc.shape[2]
    by_head = lambda r, w: pl.BlockSpec((per_step, r, w), lambda g: (g, 0, 0))
    lane = pl.BlockSpec((rows, dv * per_step), lambda g: (0, g))
    return pl.pallas_call(
        finish_kernel,
        grid=(heads // per_step,),
        in_specs=[
            by_head(rows, dk),
            by_head(rows, dv),
            by_head(dk, dv),
            lane,
            pl.BlockSpec((1, dv), lambda g: (0, 0)),
        ],
        out_specs=lane,
        out_shape=jax.ShapeDtypeStruct((rows, heads * dv), BF16),
        compiler_params=pltpu.CompilerParams(vmem_limit_bytes=32 * 2**20),
        cost_estimate=pl.CostEstimate(
            flops=2 * heads * rows * dk * dv, bytes_accessed=12 * 2**20, transcendentals=0
        ),
        name="finish_heads",
    )(qeff, oloc, states, gate, gain.reshape(1, dv))


def swap_cores(value, n):
    return lax.ppermute(value, "req", [(i, i ^ 1) for i in range(n)])


def per_device(
    tokens,
    lengths,
    in_gain,
    w_query,
    w_key,
    w_value,
    w_gate,
    w_beta,
    w_decay,
    decay_log,
    decay_bias,
    conv_query,
    conv_key,
    conv_value,
    head_gain,
    w_out,
    mlp_gain,
    w_up_gate,
    w_up,
    w_down,
):
    n = lax.axis_size("req")
    me = lax.axis_index("req")
    core = me % 2
    share_rows = tokens.shape[0]
    gathered = lax.all_gather(tokens, "mlp", axis=0, tiled=True)
    rows = gathered.shape[0]
    heads = w_beta.shape[1]
    taps = conv_query.shape[0]
    chunk = 128
    count = rows // chunk
    half = w_up.shape[1] // 2

    def weight_half(shard):
        mine = lax.dynamic_slice_in_dim(shard, core * half, half, 1)
        other = lax.dynamic_slice_in_dim(shard, (1 - core) * half, half, 1)
        theirs = swap_cores(other, n)
        first = jnp.where(core == 0, mine, theirs)
        second = jnp.where(core == 0, theirs, mine)
        both = jnp.concatenate([first, second], axis=0)
        groups = [list(range(0, n, 2)), list(range(1, n, 2))]
        return lax.all_gather(both, "req", axis=0, tiled=True, axis_index_groups=groups)

    up_gate_half = weight_half(w_up_gate)
    up_half = weight_half(w_up)
    down_half = weight_half(w_down.T)

    rim = lax.ppermute(gathered[rows - RIM :], "req", [(i, i + 1) for i in range(n - 1)])
    token_rows = gathered.astype(F32)
    normed = rms_scale(token_rows, in_gain).astype(BF16)
    gate_lin = mm(normed, w_gate).astype(BF16)
    small = mm(normed, jnp.concatenate([w_beta, w_decay], axis=1))
    rim_normed = rms_scale(rim.astype(F32), in_gain).astype(BF16)
    ext = jnp.concatenate([rim_normed, normed], axis=0)
    pq = mm(ext, w_query).astype(BF16)
    pk = mm(ext, w_key).astype(BF16)
    pv = mm(ext, w_value).astype(BF16)

    beta = jax.nn.sigmoid(small[:, :heads]).T
    gdec = (-jnp.exp(decay_log) * jax.nn.softplus(small[:, heads:] + decay_bias)).T
    piece_start = me * rows
    reach = piece_start - (taps - 1) + jnp.arange(rows + taps - 1, dtype=jnp.int32)
    seg_all = segment_of(reach, lengths)
    seg = seg_all[taps - 1 :]
    seg_chunks = seg.reshape(count, chunk)
    prior = segment_of(
        piece_start + jnp.arange(count, dtype=jnp.int32) * chunk - 1, lengths
    )
    opened = (seg_chunks == prior[:, None]).astype(F32)
    to_last = (seg_chunks == seg_chunks[:, -1:]).astype(F32)
    upper = jnp.triu(jnp.ones((chunk, chunk), F32))
    cum = jnp.dot(
        gdec.reshape(heads * count, chunk), upper, precision=lax.Precision.HIGHEST
    ).reshape(heads, count, chunk)
    start_decay = jnp.exp(cum) * opened[None]
    final_w = jnp.exp(cum[:, :, -1:] - cum) * to_last[None]
    carry = jnp.broadcast_to(start_decay[:, :, -1:], cum.shape)

    def flat(a):
        return a.reshape(heads, 1, rows)

    def shared(a):
        return jnp.broadcast_to(a.astype(F32).reshape(1, 1, rows), (heads, 1, rows))

    masks = [
        shared(seg_all[taps - 1 - s : taps - 1 - s + rows] == seg) for s in range(1, taps)
    ]
    scal = jnp.concatenate(
        [flat(beta), flat(cum), flat(start_decay), flat(final_w), flat(carry), shared(seg)]
        + masks
        + [jnp.zeros((heads, 16 - 6 - len(masks), rows), F32)],
        axis=1,
    )
    qeff, oloc, maps = local_maps(
        pq, pk, pv, conv_query, conv_key, conv_value, scal, chunk, 2
    )
    states = chain_states(maps, n)
    head_out = finish_heads(qeff, oloc, states, gate_lin, head_gain, 2)
    partial_out = mm(head_out, w_out)
    if lax.axis_size("mlp") > 1:
        partial_out = lax.psum(partial_out.astype(BF16), "mlp").astype(F32)
    resid = token_rows + partial_out
    mlp_in = rms_scale(resid, mlp_gain).astype(BF16)
    pair_in = jnp.concatenate([mlp_in, swap_cores(mlp_in, n)], axis=0)
    hidden = (jax.nn.silu(mm(pair_in, up_gate_half)) * mm(pair_in, up_half)).astype(BF16)
    down_theirs = mm_t(hidden[rows:], down_half).astype(BF16)
    from_partner = swap_cores(down_theirs, n).astype(F32)
    down = mm_t(hidden[:rows], down_half) + from_partner
    if lax.axis_size("mlp") > 1:
        down = lax.psum_scatter(
            down.astype(BF16), "mlp", scatter_dimension=0, tiled=True
        ).astype(F32)
        resid = lax.dynamic_slice_in_dim(
            resid, lax.axis_index("mlp") * share_rows, share_rows, 0
        )
    return (resid + down).astype(BF16)


def solution(mesh):
    placed = (
        P(("req", "mlp"), None),
        P(),
        P(),
        P(None, "mlp"),
        P(None, "mlp"),
        P(None, "mlp"),
        P(None, "mlp"),
        P(None, "mlp"),
        P(None, "mlp"),
        P("mlp"),
        P("mlp"),
        P(None, "mlp"),
        P(None, "mlp"),
        P(None, "mlp"),
        P(),
        P("mlp", None),
        P(),
        P("req", "mlp"),
        P("req", "mlp"),
        P("mlp", "req"),
    )
    return jax.shard_map(
        per_device, mesh=mesh, in_specs=placed, out_specs=P(("req", "mlp"), None), check_vma=False
    )
```

time: 1470 us -> 488 us (0.33)
  other arithmetic: 523 us -> 11.6 us
  matrix products: 359 us -> 103 us
  waiting for transfers between devices: 476 us -> 268 us
  local copies, waits for them, and re-layouts: 82.9 us -> 11.7 us
  Pallas kernels: 0 us -> 64 us
    another operation x4 -> x1, other arithmetic: 473 us -> 0.18 us  [the longest x2 472 us: group_parts(): jax.scipy.linalg.solve_triangular(system, jnp.transpose(targets, (1, 0, 2...]
    dot_general x90 -> x11, matrix products: 348 us -> 103 us  [the longest x8 82.5 us: mm(): return jnp.dot(a, b, preferred_element_type=F32)]
    all_gather x5 -> x3, waiting for transfers between devices: 474 us -> 259 us  [weight_half(): lax.all_gather(both, 'req', axis=0, tiled=True, axis_index_groups=groups)]
    pallas_call x0 -> x3, Pallas kernels: none -> 64 us  [the longest x1 54.7 us: local_maps(): pl.pallas_call(functools.partial(local_kernel, chunk, dk, dv), grid=(head...]
    unnamed x122 -> x42, local copies, waits for them, and re-layouts: 33.9 us -> 2.39 us
    while x57 -> x0, local copies, waits for them, and re-layouts: 25.6 us -> none
    mul x6 -> x2, other arithmetic: 20.2 us -> 0.77 us  [the longest x1 0.68 us: per_device(): final_w = jnp.exp(cum[:, :, -1:] - cum) * to_last[None]]
  transfers between devices with their start and end apart: 6 -> 9, of which waited for: 4 -> 7; matrix products, arithmetic and copies ran while one was open for 20% -> 21% of each run, Pallas kernels for 0% -> 13%
where the time goes in v1:
time: 488 us; the launch traced here: 487 us
  waiting for transfers between devices  268 us (55%)
  matrix products  103 us (21%)
  Pallas kernels  64 us (13%)
  starting transfers between devices  15 us (3%)
  between operations  13.5 us (3%)
  local copies, waits for them, and re-layouts  11.7 us (2%)
  other arithmetic  11.6 us (2%)
    all_gather x3, waiting for transfers between devices, weight_half(): lax.all_gather(both, 'req', axis=0, tiled=True, axis_index_groups=groups)  259 us
    dot_general x8, matrix products, mm(): return jnp.dot(a, b, preferred_element_type=F32)  82.5 us
    pallas_call x1, Pallas kernels, local_maps(): pl.pallas_call(functools.partial(local_kernel, chunk, dk, dv), grid=(head...  54.7 us
    dot_general x2, matrix products, mm_t(): lax.dot_general(a, b, (((1,), (1,)), ((), ())), preferred_element_type=F32)  20.4 us
    ppermute x5, starting transfers between devices, swap_cores(): return lax.ppermute(value, 'req', [(i, i ^ 1) for i in range(n)])  12.1 us
  transfers between devices with their start and end apart: 9, of which 7 were waited for; matrix products, arithmetic and copies ran while one was open for 21% of the time, Pallas kernels for 13%

profile of v1, /device:TPU:0, one launch (start us, length us, event | category | flops | bytes accessed | tf_op | source)
XLA Modules:
  0.0 487.1 jit_solution(15363490200206243486)
XLA Ops:
  6.5 1.1 constant_dynamic-slice_fusion.1
  8.2 1.3 collective-permute-done.2
  9.5 1.1 broadcast_select_fusion.3
  10.6 0.9 pad_maximum_fusion.6
  12.4 1.0 collective-permute-done.3
  13.9 1.1 bitcast_select_fusion.1
  15.0 0.9 pad_maximum_fusion.7
  16.7 2.9 collective-permute-start
  21.2 1.1 copy-done.7
  24.1 10.8 %convolution_convert_fusion.1.gate = bf16[384,4096]{1,0:T(8,128)(2,1)S(1)} fusion(bf16[384,2048]{1,0:T(8,128)(2,1)} %copy-done.7, bf16[2048,4096]{1,0:T(8,128)(2,1)} %param.26), kind=kOutput, calls=%fused_computation.2 | convolution fusion | flops 6444023808 | bytes 21495808 | tf_op jit(solution)/shard_map/dot_general | solution.py:25
  39.6 0.7 broadcast_in_dim.28
  40.3 2.1 concatenate.23.scal
  42.5 1.0 fusion.7
  43.4 1.5 fusion.9
  45.0 2.0 pad_maximum_fusion.8
  47.0 9.2 %convolution_convert_fusion.2.pk = bf16[400,2048]{1,0:T(8,128)(2,1)} fusion(bf16[2048,2048]{1,0:T(8,128)(2,1)} %param.24, bf16[384,2048]{1,0:T(8,128)(2,1)} %copy-done.7, bf16[16,2048]{1,0:T(8,128)(2,1)} %fusion.9), kind=kOutput, calls=%fused_computation.13 | convolution fusion | flops 3359539200 | bytes 11665408 | tf_op jit(solution)/shard_map/dot_general | solution.py:25
  56.2 6.9 %convolution_convert_fusion.3.pq = bf16[400,2048]{1,0:T(8,128)(2,1)S(1)} fusion(bf16[2048,2048]{1,0:T(8,128)(2,1)} %param.23, bf16[384,2048]{1,0:T(8,128)(2,1)S(1)} %copy-done.8, bf16[16,2048]{1,0:T(8,128)(2,1)S(1)} %copy-done.13), kind=kOutput, calls=%fused_computation.14 | convolution fusion | flops 3359539200 | bytes 11665408 | tf_op jit(solution)/shard_map/dot_general | solution.py:25
  63.2 11.7 %convolution_convert_fusion.pv = bf16[400,4096]{1,0:T(8,128)(2,1)} fusion(bf16[2048,4096]{1,0:T(8,128)(2,1)} %param.25, bf16[384,2048]{1,0:T(8,128)(2,1)S(1)} %copy-done.8, bf16[16,2048]{1,0:T(8,128)(2,1)S(1)} %copy-done.13), kind=kOutput, calls=%fused_computation.1 | convolution fusion | flops 6715801600 | bytes 21692416 | tf_op jit(solution)/shard_map/dot_general | solution.py:25
  74.9 54.7 %local_maps.1 = (bf16[16,384,128]{2,1,0:T(8,128)(2,1)S(1)}, bf16[16,384,256]{2,1,0:T(8,128)(2,1)}, bf16[16,128,384]{2,1,0:T(8,128)(2,1)S(1)}) custom-call(bf16[400,2048]{1,0:T(8,128)(2,1)S(1)} %convolution_convert_fusion.3.pq, bf16[400,2048]{1,0:T(8,128)(2,1)} %convolution_convert_fusion.2.pk, bf16[400,4096]{1,0:T(8,128)(2,1)} %convolution_convert_fusion.pv, ...), custom_call_target="tpu_custom_call" | custom-call | flops 12288000000 | bytes 20971520 | tf_op jit(solution)/shard_map/local_maps/pallas_call | solution.py:145
  129.7 4.4 chain_states.1.states
  134.1 4.9 %finish_heads.1 = bf16[384,4096]{1,0:T(8,128)(2,1)S(1)} custom-call(bf16[16,384,128]{2,1,0:T(8,128)(2,1)S(1)} %get-tuple-element.8.qeff, bf16[16,384,256]{2,1,0:T(8,128)(2,1)S(1)} %copy-done, bf16[16,128,256]{2,1,0:T(8,128)(2,1)S(1)} %chain_states.1.states, bf16[384,4096]{1,0:T(8,128)(2,1)S(1)} %convolution_convert_fusion.1.gate, f32[1,256]{1,0:T(1,128)S(1)} %bitcast.41), custom_call_target="tpu_custom_call" | custom-call | flops 402653184 | bytes 12582912 | tf_op jit(solution)/shard_map/finish_heads/pallas_call | solution.py:272
  139.1 10.6 %multiply_reduce_fusion = (f32[384]{0:T(512)S(1)}, f32[384,2048]{1,0:T(8,128)S(1)}) fusion(bf16[384,4096]{1,0:T(8,128)(2,1)S(1)} %finish_heads.1, bf16[4096,2048]{1,0:T(8,128)(2,1)} %param.35, bf16[384,2048]{1,0:T(8,128)(2,1)S(1)} %copy-done.6), kind=kOutput, calls=%fused_computation.12 | convolution fusion | flops 6445596160 | bytes 24643072 | tf_op jit(solution)/shard_map/dot_general | solution.py:25
  150.2 1.1 copy-done.9
  151.3 10.9 %collective-permute-start.1 = (bf16[384,2048]{1,0:T(8,128)(2,1)S(1)}, bf16[384,2048]{1,0:T(8,128)(2,1)}, u32[]{:S(2)}, u32[]{:S(2)}) collective-permute-start(bf16[384,2048]{1,0:T(8,128)(2,1)S(1)} %multiply_convert_fusion.1), channel_id=1, source_target_pairs={{0,1},{1,0},{2,3},{3,2},{4,5},{5,4},{6,7},{7,6},{8,9},{9,8},{10,11... | collective-permute-start | bytes 4718600 | tf_op jit(solution)/shard_map/ppermute | solution.py:293
  162.2 3.2 collective-permute-done.1
  165.3 16.3 %fusion.6 = f32[768,2816]{1,0:T(8,128)} fusion(bf16[2048,2816]{1,0:T(8,128)(2,1)} %all-gather.4.cloned.1.call-done, bf16[384,2048]{1,0:T(8,128)(2,1)} %collective-permute-done.1, bf16[384,2048]{1,0:T(8,128)(2,1)} %copy-done.9), kind=kOutput, calls=%fused_computation.19 | convolution fusion | flops 8864661504 | bytes 23330816 | tf_op jit(solution)/shard_map/dot_general | solution.py:25
  181.6 129.8 %all-gather.6.cloned.1.call-done = bf16[2048,2816]{1,0:T(8,128)(2,1)} async-done(((bf16[128,2816]{1,0:T(8,128)(2,1)}), bf16[2048,2816]{1,0:T(8,128)(2,1)}) %all-gather.6.cloned.1.call-update) | async-done | bytes 11534352 | tf_op jit(solution)/shard_map/all_gather | solution.py:338
  311.4 16.4 %multiply_convert_fusion = bf16[768,2816]{1,0:T(8,128)(2,1)} fusion(f32[768,2816]{1,0:T(8,128)} %fusion.6, bf16[2048,2816]{1,0:T(8,128)(2,1)} %all-gather.6.cloned.1.call-done, bf16[384,2048]{1,0:T(8,128)(2,1)} %collective-permute-done.1, bf16[384,2048]{1,0:T(8,128)(2,1)} %copy-done.9), kind=kOutput, calls=%fused_computation | convolution fusion | flops 8877637632 | bytes 27656192 | tf_op jit(solution)/shard_map/dot_general | solution.py:25
  327.8 128.9 %all-gather.8.cloned.1.call-done = bf16[2048,2816]{1,0:T(8,128)(2,1)} async-done(((bf16[128,2816]{1,0:T(8,128)(2,1)}), bf16[2048,2816]{1,0:T(8,128)(2,1)}) %all-gather.8.cloned.1.call-update) | async-done | bytes 11534352 | tf_op jit(solution)/shard_map/all_gather | solution.py:338
  456.7 9.6 %convolution_convert_fusion.4 = bf16[384,2048]{1,0:T(8,128)(2,1)S(1)} fusion(bf16[2048,2816]{1,0:T(8,128)(2,1)} %all-gather.8.cloned.1.call-done, bf16[768,2816]{1,0:T(8,128)(2,1)} %multiply_convert_fusion), kind=kOutput, calls=%fused_computation.15 | convolution fusion | flops 4429971456 | bytes 15269888 | tf_op jit(solution)/shard_map/dot_general | solution.py:29
  466.3 3.4 collective-permute-done.5
  469.7 10.8 %add_convert_fusion = bf16[384,2048]{1,0:T(8,128)(2,1)} fusion(f32[384,2048]{1,0:T(8,128)S(1)} %get-tuple-element.31, bf16[384,2048]{1,0:T(8,128)(2,1)S(1)} %collective-permute-done.5, bf16[2048,2816]{1,0:T(8,128)(2,1)} %all-gather.8.cloned.1.call-done, bf16[768,2816]{1,0:T(8,128)(2,1)} %multiply_convert_fusion), kind=kOutput, calls=%fused_computation.10 | convolution fusion | flops 4432330752 | bytes 19988480 | tf_op jit(solution)/shard_map/dot_general | solution.py:29
  (96 shorter events, 11.1 us)
Async XLA Ops:
  6.5 5.1 %copy-start.11 = (bf16[64,5632]{1,0:T(8,128)(2,1)S(1)}, bf16[64,5632]{1,0:T(8,128)(2,1)}, u32[]{:S(2)}) copy-start(bf16[64,5632]{1,0:T(8,128)(2,1)} %param.38) | copy-start | bytes 2162692
  6.5 5.6 %copy-start.10 = (bf16[5632,64]{0,1:T(8,128)(2,1)S(1)}, bf16[5632,64]{0,1:T(8,128)(2,1)}, u32[]{:S(2)}) copy-start(bf16[5632,64]{0,1:T(8,128)(2,1)} %param.39) | copy-start | bytes 2162692
  6.5 158.8 %all-gather.4.cloned.1.call-start = ((), (), s32[]{:S(2)}) async-start(), calls=%async_computation | async-start | bytes 12255232 | tf_op jit(solution)/shard_map/all_gather | solution.py:338
  7.7 1.8 collective-permute-start.2
  11.5 4.5 copy-start.5
  11.5 8.0 %copy-start.19 = (s32[4]{0:T(128)S(1)}, s32[4]{0:T(128)}, u32[]{:S(2)}) copy-start(s32[4]{0:T(128)} %param.21) | copy-start | bytes 52
  11.6 299.8 %all-gather.6.cloned.1.call-start = ((), (), s32[]{:S(2)}) async-start(), calls=%async_computation.1 | async-start | bytes 12255232 | tf_op jit(solution)/shard_map/all_gather | solution.py:338
  11.7 1.7 collective-permute-start.3
  12.1 8.4 %copy-start.20 = (f32[16]{0:T(128)S(1)}, f32[16]{0:T(128)}, u32[]{:S(2)}) copy-start(f32[16]{0:T(128)} %param.29) | copy-start | bytes 196
  12.1 8.4 %copy-start.16 = (f32[2048]{0:T(1024)S(1)}, f32[2048]{0:T(1024)}, u32[]{:S(2)}) copy-start(f32[2048]{0:T(1024)} %param.22) | copy-start | bytes 24580
  12.2 1.8 collective-permute-start.4
  16.0 6.3 %copy-start.14 = (bf16[2048,16]{0,1:T(8,128)(2,1)S(1)}, bf16[2048,16]{0,1:T(8,128)(2,1)}, u32[]{:S(2)}) copy-start(bf16[2048,16]{0,1:T(8,128)(2,1)} %param.28) | copy-start | bytes 196612
  16.0 6.3 %copy-start.15 = (bf16[2048,16]{0,1:T(8,128)(2,1)S(1)}, bf16[2048,16]{0,1:T(8,128)(2,1)}, u32[]{:S(2)}) copy-start(bf16[2048,16]{0,1:T(8,128)(2,1)} %param.27) | copy-start | bytes 196612
  16.0 440.7 %all-gather.8.cloned.1.call-start = ((), (), s32[]{:S(2)}) async-start(), calls=%async_computation.2 | async-start | bytes 12255232 | tf_op jit(solution)/shard_map/all_gather | solution.py:338
  16.7 25.8 %collective-permute-start = (bf16[16,2048]{1,0:T(8,128)(2,1)}, bf16[16,2048]{1,0:T(8,128)(2,1)}, u32[]{:S(2)}, u32[]{:S(2)}) collective-permute-start(bf16[16,2048]{1,0:T(8,128)(2,1)} %slice.43), channel_id=1, source_target_pairs={{0,1},{1,2},{2,3},{3,4},{4,5},{5,6},{6,7},{7,8},{8,9},{9,10},{10,1... | collective-permute-start | bytes 196616 | tf_op jit(solution)/shard_map/ppermute | solution.py:344
  20.2 2.7 copy-start.18
  21.1 1.1 copy-start.7
  23.2 11.7 %copy-start.12 = (f32[48,128]{1,0:T(8,128)}, f32[48,128]{1,0:T(8,128)S(1)}, u32[]{:S(2)}) copy-start(f32[48,128]{1,0:T(8,128)S(1)} %fusion.14) | copy-start | bytes 73732
  47.0 9.2 %copy-start.8 = (bf16[384,2048]{1,0:T(8,128)(2,1)S(1)}, bf16[384,2048]{1,0:T(8,128)(2,1)}, u32[]{:S(2)}) copy-start(bf16[384,2048]{1,0:T(8,128)(2,1)} %copy-done.7) | copy-start | bytes 4718596
  47.0 9.2 %copy-start.13 = (bf16[16,2048]{1,0:T(8,128)(2,1)S(1)}, bf16[16,2048]{1,0:T(8,128)(2,1)}, u32[]{:S(2)}) copy-start(bf16[16,2048]{1,0:T(8,128)(2,1)} %fusion.9) | copy-start | bytes 196612
  63.2 11.8 %copy-start.2 = (f32[4,4096]{1,0:T(4,128)S(1)}, f32[4,4096]{1,0:T(4,128)}, u32[]{:S(2)}) copy-start(f32[4,4096]{1,0:T(4,128)} %tv.1) | copy-start | bytes 196612
  63.2 11.8 %copy-start.3 = (f32[4,2048]{1,0:T(4,128)S(1)}, f32[4,2048]{1,0:T(4,128)}, u32[]{:S(2)}) copy-start(f32[4,2048]{1,0:T(4,128)} %tq.1) | copy-start | bytes 98308
  63.2 11.8 %copy-start.4 = (f32[4,2048]{1,0:T(4,128)S(1)}, f32[4,2048]{1,0:T(4,128)}, u32[]{:S(2)}) copy-start(f32[4,2048]{1,0:T(4,128)} %tk.1) | copy-start | bytes 98308
  129.7 4.4 copy-start
  129.7 4.4 copy-start.1
  134.1 4.9 %copy-start.6 = (bf16[384,2048]{1,0:T(8,128)(2,1)S(1)}, bf16[384,2048]{1,0:T(8,128)(2,1)}, u32[]{:S(2)}) copy-start(bf16[384,2048]{1,0:T(8,128)(2,1)} %param.20) | copy-start | bytes 4718596
  139.0 10.6 %copy-start.17 = (f32[2048]{0:T(1024)S(1)}, f32[2048]{0:T(1024)}, u32[]{:S(2)}) copy-start(f32[2048]{0:T(1024)} %param.36) | copy-start | bytes 24580
  150.2 1.1 copy-start.9
  151.3 14.0 %collective-permute-start.1 = (bf16[384,2048]{1,0:T(8,128)(2,1)S(1)}, bf16[384,2048]{1,0:T(8,128)(2,1)}, u32[]{:S(2)}, u32[]{:S(2)}) collective-permute-start(bf16[384,2048]{1,0:T(8,128)(2,1)S(1)} %multiply_convert_fusion.1), channel_id=1, source_target_pairs={{0,1},{1,0},{2,3},{3,2},{4,5},{5,4},{6,7},{7,6},{8,9},{9,8},{10,11... | collective-permute-start | bytes 4718600 | tf_op jit(solution)/shard_map/ppermute | solution.py:293
  466.3 3.5 collective-permute-start.5
Sparse Core Ops, SparseCore 0:
  11.7 144.8 all-gather.3
  159.3 152.0 all-gather.5
  314.1 142.5 all-gather.7

commit v2 on v1

--- a/solution.py
+++ b/solution.py
@@ -173,77 +173,130 @@
     )(pq, pk, pv, tq, tk, tv, scal)
 
 
-def chain_kernel(n, dk, maps, states, landing, outgoing, send_sem, recv_sem):
+def chain_kernel(
+    n, dk, maps, states, theirs, first, joined, landing, outgoing, to_peer, from_peer,
+    swap_send, swap_recv, send_sem, recv_sem, peer_send, peer_recv
+):
     me = lax.axis_index("req")
-    heads = maps.shape[0]
+    core = lax.rem(me, 2)
+    peer = me + 1 - 2 * core
+    per_core = joined.shape[0]
+    has_left, has_right = me >= 2, me < n - 2
     barrier = pltpu.get_barrier_semaphore()
-    has_left, has_right = me > 0, me < n - 1
+    mesh_id = pl.DeviceIdType.MESH
+    pl.semaphore_signal(barrier, inc=1, device_id={"req": peer}, device_id_type=mesh_id)
 
     @pl.when(has_left)
     def _():
-        pl.semaphore_signal(
-            barrier, inc=1, device_id={"req": me - 1}, device_id_type=pl.DeviceIdType.MESH
-        )
-
-    @pl.when(has_right)
-    def _():
-        pl.semaphore_wait(barrier, 1)
-
-    def copy(h):
+        pl.semaphore_signal(barrier, inc=1, device_id={"req": me - 2}, device_id_type=mesh_id)
+
+    pl.semaphore_wait(barrier, 1 + has_right.astype(jnp.int32))
+    own_base = core * per_core
+    peer_base = (1 - core) * per_core
+
+    swap = pltpu.make_async_remote_copy(
+        src_ref=maps.at[pl.ds(peer_base, per_core)],
+        dst_ref=theirs,
+        send_sem=swap_send,
+        recv_sem=swap_recv,
+        device_id={"req": peer},
+        device_id_type=mesh_id,
+    )
+    swap.start()
+    swap.wait_recv()
+
+    def join(h, carry):
+        mine, other = maps[own_base + h], theirs[h]
+        early = jnp.where(core == 0, mine, other)
+        late = jnp.where(core == 0, other, mine)
+        both = mm(late[:, :dk], early)
+        first[h] = early
+        joined[h, :, :dk] = both[:, :dk].astype(BF16)
+        joined[h, :, dk:] = (both[:, dk:] + late[:, dk:].astype(F32)).astype(BF16)
+        return carry
+
+    lax.fori_loop(0, per_core, join, 0)
+
+    def onward_copy(h):
         return pltpu.make_async_remote_copy(
             src_ref=outgoing.at[h],
             dst_ref=landing.at[h],
             send_sem=send_sem.at[h],
             recv_sem=recv_sem.at[h],
-            device_id={"req": me + 1},
-            device_id_type=pl.DeviceIdType.MESH,
+            device_id={"req": me + 2},
+            device_id_type=mesh_id,
+        )
+
+    def peer_copy(h):
+        return pltpu.make_async_remote_copy(
+            src_ref=to_peer.at[h],
+            dst_ref=from_peer.at[h],
+            send_sem=peer_send.at[h],
+            recv_sem=peer_recv.at[h],
+            device_id={"req": peer},
+            device_id_type=mesh_id,
         )
 
     def one(h, carry):
         @pl.when(has_left)
         def _():
-            copy(h).wait_recv()
-            coming = landing[h]
-            states[h] = coming
-            onward = mm(maps[h, :, :dk], coming) + maps[h, :, dk:].astype(F32)
-            outgoing[h] = onward.astype(BF16)
-
-        @pl.when(me == 0)
+            onward_copy(h).wait_recv()
+
+        @pl.when(jnp.logical_not(has_left))
         def _():
-            states[h] = jnp.zeros(states.shape[1:], BF16)
-            outgoing[h] = maps[h, :, dk:]
+            landing[h] = jnp.zeros(landing.shape[1:], BF16)
+
+        coming = landing[h]
 
         @pl.when(has_right)
         def _():
-            copy(h).start()
-
+            onward = mm(joined[h, :, :dk], coming) + joined[h, :, dk:].astype(F32)
+            outgoing[h] = onward.astype(BF16)
+            onward_copy(h).start()
+
+        middle = (mm(first[h, :, :dk], coming) + first[h, :, dk:].astype(F32)).astype(BF16)
+        states[own_base + h] = jnp.where(core == 0, coming, middle)
+        to_peer[h] = jnp.where(core == 0, middle, coming)
+        peer_copy(h).start()
         return carry
 
-    lax.fori_loop(0, heads, one, 0)
+    lax.fori_loop(0, per_core, one, 0)
+
+    def collect(h, carry):
+        peer_copy(h).wait_recv()
+        states[peer_base + h] = from_peer[h]
+        peer_copy(h).wait_send()
+        return carry
+
+    lax.fori_loop(0, per_core, collect, 0)
 
     def drain(h, carry):
-        copy(h).wait_send()
+        onward_copy(h).wait_send()
         return carry
 
     @pl.when(has_right)
     def _():
-        lax.fori_loop(0, heads, drain, 0)
+        lax.fori_loop(0, per_core, drain, 0)
+
+    swap.wait_send()
 
 
 def chain_states(maps, n):
     heads, dk, width = maps.shape
     dv = width - dk
+    per_core = heads // 2
+    map_buf = pltpu.VMEM((per_core, dk, width), BF16)
+    state_buf = pltpu.VMEM((per_core, dk, dv), BF16)
+    sems = pltpu.SemaphoreType.DMA((per_core,))
     return pl.pallas_call(
         functools.partial(chain_kernel, n, dk),
         in_specs=[pl.BlockSpec(memory_space=pltpu.VMEM)],
         out_specs=pl.BlockSpec(memory_space=pltpu.VMEM),
         out_shape=jax.ShapeDtypeStruct((heads, dk, dv), BF16),
-        scratch_shapes=[
-            pltpu.VMEM((heads, dk, dv), BF16),
-            pltpu.VMEM((heads, dk, dv), BF16),
-            pltpu.SemaphoreType.DMA((heads,)),
-            pltpu.SemaphoreType.DMA((heads,)),
-        ],
+        scratch_shapes=[map_buf] * 3
+        + [state_buf] * 4
+        + [pltpu.SemaphoreType.DMA] * 2
+        + [sems] * 4,
         compiler_params=pltpu.CompilerParams(
             collective_id=0, has_side_effects=True, vmem_limit_bytes=32 * 2**20
         ),
@@ -289,8 +342,8 @@
     )(qeff, oloc, states, gate, gain.reshape(1, dv))
 
 
-def swap_cores(value, n):
-    return lax.ppermute(value, "req", [(i, i ^ 1) for i in range(n)])
+def swapped(value, n, bits):
+    return lax.ppermute(value, "req", [(i, i ^ bits) for i in range(n)])
 
 
 def per_device(
@@ -317,7 +370,6 @@
 ):
     n = lax.axis_size("req")
     me = lax.axis_index("req")
-    core = me % 2
     share_rows = tokens.shape[0]
     gathered = lax.all_gather(tokens, "mlp", axis=0, tiled=True)
     rows = gathered.shape[0]
@@ -325,21 +377,28 @@
     taps = conv_query.shape[0]
     chunk = 128
     count = rows // chunk
-    half = w_up.shape[1] // 2
-
-    def weight_half(shard):
-        mine = lax.dynamic_slice_in_dim(shard, core * half, half, 1)
-        other = lax.dynamic_slice_in_dim(shard, (1 - core) * half, half, 1)
-        theirs = swap_cores(other, n)
-        first = jnp.where(core == 0, mine, theirs)
-        second = jnp.where(core == 0, theirs, mine)
-        both = jnp.concatenate([first, second], axis=0)
-        groups = [list(range(0, n, 2)), list(range(1, n, 2))]
-        return lax.all_gather(both, "req", axis=0, tiled=True, axis_index_groups=groups)
-
-    up_gate_half = weight_half(w_up_gate)
-    up_half = weight_half(w_up)
-    down_half = weight_half(w_down.T)
+    group = 4
+    spot = me % group
+    quarter = w_up.shape[1] // group
+    shards = jnp.concatenate([w_up_gate, w_up, w_down.T], axis=0)
+    depth = w_up.shape[0]
+    pieces = jnp.zeros((group,) + (shards.shape[0], quarter), BF16)
+    for d in range(group):
+        piece = lax.dynamic_slice_in_dim(shards, (spot ^ d) * quarter, quarter, 1)
+        if d:
+            piece = swapped(piece, n, d)
+        pieces = lax.dynamic_update_slice_in_dim(pieces, piece[None], spot ^ d, 0)
+    members = [list(range(k, n, group)) for k in range(group)]
+    up_gate_part, up_part, down_part = [
+        lax.all_gather(
+            pieces[:, m * depth : (m + 1) * depth].reshape(group * depth, quarter),
+            "req",
+            axis=0,
+            tiled=True,
+            axis_index_groups=members,
+        )
+        for m in range(3)
+    ]
 
     rim = lax.ppermute(gathered[rows - RIM :], "req", [(i, i + 1) for i in range(n - 1)])
     token_rows = gathered.astype(F32)
@@ -372,20 +431,18 @@
     final_w = jnp.exp(cum[:, :, -1:] - cum) * to_last[None]
     carry = jnp.broadcast_to(start_decay[:, :, -1:], cum.shape)
 
-    def flat(a):
-        return a.reshape(heads, 1, rows)
-
     def shared(a):
-        return jnp.broadcast_to(a.astype(F32).reshape(1, 1, rows), (heads, 1, rows))
-
-    masks = [
+        return jnp.broadcast_to(a.astype(F32)[None], (heads, rows))
+
+    fields = [beta] + [a.reshape(heads, rows) for a in (cum, start_decay, final_w, carry)]
+    fields.append(shared(seg))
+    fields += [
         shared(seg_all[taps - 1 - s : taps - 1 - s + rows] == seg) for s in range(1, taps)
     ]
-    scal = jnp.concatenate(
-        [flat(beta), flat(cum), flat(start_decay), flat(final_w), flat(carry), shared(seg)]
-        + masks
-        + [jnp.zeros((heads, 16 - 6 - len(masks), rows), F32)],
-        axis=1,
+    fields.append(jnp.zeros(((16 - len(fields)) * heads, rows), F32))
+    scal = jnp.transpose(
+        lax.optimization_barrier(jnp.concatenate(fields, axis=0)).reshape(16, heads, rows),
+        (1, 0, 2),
     )
     qeff, oloc, maps = local_maps(
         pq, pk, pv, conv_query, conv_key, conv_value, scal, chunk, 2
@@ -397,11 +454,20 @@
         partial_out = lax.psum(partial_out.astype(BF16), "mlp").astype(F32)
     resid = token_rows + partial_out
     mlp_in = rms_scale(resid, mlp_gain).astype(BF16)
-    pair_in = jnp.concatenate([mlp_in, swap_cores(mlp_in, n)], axis=0)
-    hidden = (jax.nn.silu(mm(pair_in, up_gate_half)) * mm(pair_in, up_half)).astype(BF16)
-    down_theirs = mm_t(hidden[rows:], down_half).astype(BF16)
-    from_partner = swap_cores(down_theirs, n).astype(F32)
-    down = mm_t(hidden[:rows], down_half) + from_partner
+    far_b = swapped(mlp_in, n, 2)
+    near = jnp.concatenate([mlp_in, swapped(mlp_in, n, 1)], axis=0)
+    far = jnp.concatenate([far_b, swapped(far_b, n, 1)], axis=0)
+
+    def hidden_of(x):
+        return (jax.nn.silu(mm(x, up_gate_part)) * mm(x, up_part)).astype(BF16)
+
+    near_hidden = hidden_of(near)
+    far_down = mm_t(hidden_of(far), down_part)
+    far_chip = far_down[:rows] + swapped(far_down[rows:].astype(BF16), n, 1).astype(F32)
+    from_far = swapped(far_chip.astype(BF16), n, 2).astype(F32)
+    near_down = mm_t(near_hidden, down_part)
+    from_near = swapped(near_down[rows:].astype(BF16), n, 1).astype(F32)
+    down = near_down[:rows] + from_near + from_far
     if lax.axis_size("mlp") > 1:
         down = lax.psum_scatter(
             down.astype(BF16), "mlp", scatter_dimension=0, tiled=True

time: 488 us -> 444 us (0.910)
  waiting for transfers between devices: 268 us -> 190 us
  local copies, waits for them, and re-layouts: 11.7 us -> 26.6 us
  Pallas kernels: 64 us -> 76.6 us
    all_gather x3, waiting for transfers between devices: 259 us -> 99.7 us  [per_device(): lax.all_gather(pieces[:, m * depth:(m + 1) * depth].reshape(group * depth...]
    ppermute x5 -> x9, waiting for transfers between devices: 9.43 us -> 90.7 us  [swapped(): return lax.ppermute(value, 'req', [(i, i ^ bits) for i in range(n)])]
    dot_general x2, matrix products: 20.4 us -> 38.6 us  [mm_t(): lax.dot_general(a, b, (((1,), (1,)), ((), ())), preferred_element_type=F32)]
    dot_general x8, matrix products: 82.5 us -> 68.2 us  [mm(): return jnp.dot(a, b, preferred_element_type=F32)]
    pallas_call x1, Pallas kernels: 4.4 us -> 17 us  [chain_states(): pl.pallas_call(functools.partial(chain_kernel, n, dk), in_specs=[pl.Block...]
    slice x0 -> x3, local copies, waits for them, and re-layouts: none -> 8.4 us  [the longest x1 3.28 us: per_device(): far_down[rows:].astype(BF16)]
    dynamic_update_slice x0 -> x4, local copies, waits for them, and re-layouts: none -> 6.53 us  [per_device(): pieces = lax.dynamic_update_slice_in_dim(pieces, piece[None], spot ^ d, 0)]
    convert_element_type x2 -> x4, other arithmetic: 0.15 us -> 5.56 us  [the longest x1 3.17 us: per_device(): from_far = swapped(far_chip.astype(BF16), n, 2).astype(F32)]
  transfers between devices with their start and end apart: 9 -> 13, of which waited for: 7 -> 7; matrix products, arithmetic and copies ran while one was open for 21% -> 30% of each run, Pallas kernels for 13% -> 17%
where the time goes in v2:
time: 444 us; the launch traced here: 441 us
  waiting for transfers between devices  190 us (43%)
  matrix products  107 us (24%)
  Pallas kernels  76.6 us (17%)
  local copies, waits for them, and re-layouts  26.6 us (6%)
  between operations  13.7 us (3%)
  starting transfers between devices  13.6 us (3%)
  other arithmetic  12.7 us (3%)
    all_gather x3, waiting for transfers between devices, per_device(): lax.all_gather(pieces[:, m * depth:(m + 1) * depth].reshape(group * depth...  99.7 us
    ppermute x9, waiting for transfers between devices, swapped(): return lax.ppermute(value, 'req', [(i, i ^ bits) for i in range(n)])  90.7 us
    dot_general x8, matrix products, mm(): return jnp.dot(a, b, preferred_element_type=F32)  68.2 us
    pallas_call x1, Pallas kernels, local_maps(): pl.pallas_call(functools.partial(local_kernel, chunk, dk, dv), grid=(head...  54.7 us
    dot_general x2, matrix products, mm_t(): lax.dot_general(a, b, (((1,), (1,)), ((), ())), preferred_element_type=F32)  38.6 us
    pallas_call x1, Pallas kernels, chain_states(): pl.pallas_call(functools.partial(chain_kernel, n, dk), in_specs=[pl.Block...  17 us
    ppermute x9, starting transfers between devices, swapped(): return lax.ppermute(value, 'req', [(i, i ^ bits) for i in range(n)])  10.6 us
  transfers between devices with their start and end apart: 13, of which 7 were waited for; matrix products, arithmetic and copies ran while one was open for 30% of the time, Pallas kernels for 17%

profile of v2, /device:TPU:0, one launch (start us, length us, event | category | flops | bytes accessed | tf_op | source)
XLA Modules:
  0.0 440.7 jit_solution(13009959898401038306)
XLA Ops:
  6.5 1.7 pad_maximum_fusion.1
  9.6 2.5 collective-permute-start.3
  14.6 1.9 bitcast_dynamic-update-slice_fusion.2
  16.5 8.8 %collective-permute-done.3 = bf16[192,1408]{1,0:T(8,128)(2,1)} collective-permute-done((bf16[192,1408]{1,0:T(8,128)(2,1)S(1)}, bf16[192,1408]{1,0:T(8,128)(2,1)}, u32[]{:S(2)}, u32[]{:S(2)}) %collective-permute-start.3) | collective-permute-done | bytes 540704 | tf_op jit(solution)/shard_map/ppermute | solution.py:346
  25.3 1.9 bitcast_dynamic-update-slice_fusion.1
  27.2 9.3 %collective-permute-done.4 = bf16[192,1408]{1,0:T(8,128)(2,1)} collective-permute-done((bf16[192,1408]{1,0:T(8,128)(2,1)S(1)}, bf16[192,1408]{1,0:T(8,128)(2,1)}, u32[]{:S(2)}, u32[]{:S(2)}) %collective-permute-start.4) | collective-permute-done | bytes 540704 | tf_op jit(solution)/shard_map/ppermute | solution.py:346
  36.5 1.9 bitcast_dynamic-update-slice_fusion
  38.4 3.0 fusion.49
  42.2 2.7 collective-permute-start
  50.1 12.8 %convolution_convert_fusion.1.gate = bf16[384,4096]{1,0:T(8,128)(2,1)S(1)} fusion(bf16[384,2048]{1,0:T(8,128)(2,1)} %copy-done.11, bf16[2048,4096]{1,0:T(8,128)(2,1)} %param.26), kind=kOutput, calls=%fused_computation.1 | convolution fusion | flops 6444023808 | bytes 21495808 | tf_op jit(solution)/shard_map/dot_general | solution.py:25
  65.2 7.1 %convolution_convert_fusion.3.pq = bf16[400,2048]{1,0:T(8,128)(2,1)S(1)} fusion(bf16[2048,2048]{1,0:T(8,128)(2,1)} %param.23, bf16[384,2048]{1,0:T(8,128)(2,1)S(1)} %copy-done.12, bf16[16,2048]{1,0:T(8,128)(2,1)S(1)} %fusion.15), kind=kOutput, calls=%fused_computation.22 | convolution fusion | flops 3359539200 | bytes 11665408 | tf_op jit(solution)/shard_map/dot_general | solution.py:25
  72.3 4.7 %convolution_convert_fusion.2.pk = bf16[400,2048]{1,0:T(8,128)(2,1)} fusion(bf16[2048,2048]{1,0:T(8,128)(2,1)S(1)} %bitcast.81, bf16[384,2048]{1,0:T(8,128)(2,1)S(1)} %copy-done.12, bf16[16,2048]{1,0:T(8,128)(2,1)S(1)} %fusion.15), kind=kOutput, calls=%fused_computation.21 | convolution fusion | flops 3359539200 | bytes 11665408 | tf_op jit(solution)/shard_map/dot_general | solution.py:25
  77.0 11.7 %convolution_convert_fusion.pv = bf16[400,4096]{1,0:T(8,128)(2,1)} fusion(bf16[2048,4096]{1,0:T(8,128)(2,1)} %param.25, bf16[384,2048]{1,0:T(8,128)(2,1)S(1)} %copy-done.12, bf16[16,2048]{1,0:T(8,128)(2,1)S(1)} %fusion.15), kind=kOutput, calls=%fused_computation | convolution fusion | flops 6715801600 | bytes 21692416 | tf_op jit(solution)/shard_map/dot_general | solution.py:25
  88.8 54.7 %local_maps.1 = (bf16[16,384,128]{2,1,0:T(8,128)(2,1)S(1)}, bf16[16,384,256]{2,1,0:T(8,128)(2,1)}, bf16[16,128,384]{2,1,0:T(8,128)(2,1)S(1)}) custom-call(bf16[400,2048]{1,0:T(8,128)(2,1)S(1)} %convolution_convert_fusion.3.pq, bf16[400,2048]{1,0:T(8,128)(2,1)} %convolution_convert_fusion.2.pk, bf16[400,4096]{1,0:T(8,128)(2,1)} %convolution_convert_fusion.pv, ...), custom_call_target="tpu_custom_call" | custom-call | flops 12288000000 | bytes 20971520 | tf_op jit(solution)/shard_map/local_maps/pallas_call | solution.py:145
  147.3 17.0 %chain_states.1.states = bf16[16,128,256]{2,1,0:T(8,128)(2,1)S(1)} custom-call(bf16[16,128,384]{2,1,0:T(8,128)(2,1)S(1)} %copy-done.8), custom_call_target="tpu_custom_call" | custom-call | flops 60000002048 | bytes 3145728 | tf_op jit(solution)/shard_map/chain_states/pallas_call | solution.py:291
  164.3 4.9 %finish_heads.1 = bf16[384,4096]{1,0:T(8,128)(2,1)S(1)} custom-call(bf16[16,384,128]{2,1,0:T(8,128)(2,1)S(1)} %copy-done.2, bf16[16,384,256]{2,1,0:T(8,128)(2,1)S(1)} %copy-done, bf16[16,128,256]{2,1,0:T(8,128)(2,1)S(1)} %chain_states.1.states, bf16[384,4096]{1,0:T(8,128)(2,1)S(1)} %convolution_convert_fusion.1.gate, f32[1,256]{1,0:T(1,128)S(1)} %bitcast.70), custom_call_target="tpu_custom_call" | custom-call | flops 402653184 | bytes 12582912 | tf_op jit(solution)/shard_map/finish_heads/pallas_call | solution.py:325
  169.2 10.6 %multiply_reduce_fusion = (f32[384]{0:T(512)S(1)}, f32[384,2048]{1,0:T(8,128)S(1)}) fusion(bf16[384,4096]{1,0:T(8,128)(2,1)S(1)} %finish_heads.1, bf16[4096,2048]{1,0:T(8,128)(2,1)} %param.35, bf16[384,2048]{1,0:T(8,128)(2,1)S(1)} %copy-done.10), kind=kOutput, calls=%fused_computation.20 | convolution fusion | flops 6445596160 | bytes 24643072 | tf_op jit(solution)/shard_map/dot_general | solution.py:25
  179.8 1.7 multiply_convert_fusion.2
  181.5 4.9 %collective-permute-start.6 = (bf16[384,2048]{1,0:T(8,128)(2,1)}, bf16[384,2048]{1,0:T(8,128)(2,1)S(1)}, u32[]{:S(2)}, u32[]{:S(2)}) collective-permute-start(bf16[384,2048]{1,0:T(8,128)(2,1)} %multiply_convert_fusion.2), channel_id=1, source_target_pairs={{0,2},{1,3},{2,0},{3,1},{4,6},{5,7},{6,4},{7,5},{8,10},{9,11},{10,... | collective-permute-start | bytes 4718600 | tf_op jit(solution)/shard_map/ppermute | solution.py:346
  186.4 34.0 %collective-permute-done.6 = bf16[384,2048]{1,0:T(8,128)(2,1)S(1)} collective-permute-done((bf16[384,2048]{1,0:T(8,128)(2,1)}, bf16[384,2048]{1,0:T(8,128)(2,1)S(1)}, u32[]{:S(2)}, u32[]{:S(2)}) %collective-permute-start.6) | collective-permute-done | bytes 1572896 | tf_op jit(solution)/shard_map/ppermute | solution.py:346
  222.2 3.8 collective-permute-done.7
  227.2 10.0 %fusion.52 = f32[768,1408]{1,0:T(8,128)} fusion(bf16[768,2048]{1,0:T(8,128)(2,1)} %constant_dynamic-update-slice_fusion.9, bf16[2048,1408]{1,0:T(8,128)(2,1)} %all-gather.4.cloned.1.call-done), kind=kOutput, calls=%fused_computation.117 | convolution fusion | flops 4429185024 | bytes 13238272 | tf_op jit(solution)/shard_map/dot_general | solution.py:25
  237.3 3.9 all-gather.8.cloned.1.call-done
  241.2 95.8 %all-gather.6.cloned.1.call-done = bf16[2048,1408]{1,0:T(8,128)(2,1)} async-done(((bf16[256,1408]{1,0:T(8,128)(2,1)}), bf16[2048,1408]{1,0:T(8,128)(2,1)}) %all-gather.6.cloned.1.call-update) | async-done | bytes 5767184 | tf_op jit(solution)/shard_map/all_gather | solution.py:393
  337.0 19.2 %fusion.8 = f32[768,2048]{1,0:T(8,128)} fusion(bf16[2048,1408]{1,0:T(8,128)(2,1)} %all-gather.8.cloned.1.call-done, f32[768,1408]{1,0:T(8,128)} %fusion.52, bf16[768,2048]{1,0:T(8,128)(2,1)} %constant_dynamic-update-slice_fusion.9, bf16[2048,1408]{1,0:T(8,128)(2,1)} %all-gather.6.cloned.1.call-done), kind=kOutput, calls=%fused_computation.24 | convolution fusion | flops 8864858112 | bytes 25296896 | tf_op jit(solution)/shard_map/dot_general | solution.py:29
  356.2 3.3 slice.138
  359.4 10.7 %fusion.11 = f32[768,1408]{1,0:T(8,128)} fusion(bf16[2048,1408]{1,0:T(8,128)(2,1)} %all-gather.6.cloned.1.call-done, bf16[384,2048]{1,0:T(8,128)(2,1)} %collective-permute-done.1, bf16[384,2048]{1,0:T(8,128)(2,1)} %multiply_convert_fusion.2), kind=kOutput, calls=%fused_computation.28 | convolution fusion | flops 4435476480 | bytes 13238272 | tf_op jit(solution)/shard_map/dot_general | solution.py:25
  370.1 19.4 %fusion.7 = f32[768,2048]{1,0:T(8,128)} fusion(bf16[2048,1408]{1,0:T(8,128)(2,1)} %all-gather.8.cloned.1.call-done, f32[768,1408]{1,0:T(8,128)} %fusion.11, bf16[2048,1408]{1,0:T(8,128)(2,1)} %all-gather.4.cloned.1.call-done, bf16[384,2048]{1,0:T(8,128)(2,1)} %collective-permute-done.1, bf16[384,2048]{1,0:T(8,128)(2,1)} %multiply_convert_fusion.2), kind=kOutput, calls=%fused_computation.23 | convolution fusion | flops 8871149568 | bytes 25296896 | tf_op jit(solution)/shard_map/dot_general | solution.py:29
  389.6 2.1 slice.139
  392.3 3.2 fusion.3
  397.0 34.8 %collective-permute-done.9 = bf16[384,2048]{1,0:T(8,128)(2,1)S(1)} collective-permute-done((bf16[384,2048]{1,0:T(8,128)(2,1)S(1)}, bf16[384,2048]{1,0:T(8,128)(2,1)S(1)}, u32[]{:S(2)}, u32[]{:S(2)}) %collective-permute-start.9) | collective-permute-done | bytes 1572896 | tf_op jit(solution)/shard_map/ppermute | solution.py:346
  431.7 2.2 fusion.6
  (117 shorter events, 20.8 us)
Async XLA Ops:
  6.5 220.7 %all-gather.4.cloned.1.call-start = ((), (), s32[]{:S(2)}) async-start(), calls=%async_computation | async-start | bytes 6488064 | tf_op jit(solution)/shard_map/all_gather | solution.py:393
  9.2 5.4 %collective-permute-start.2 = (bf16[192,1408]{1,0:T(8,128)(2,1)}, bf16[192,1408]{1,0:T(8,128)(2,1)}, u32[]{:S(2)}, u32[]{:S(2)}) collective-permute-start(bf16[192,1408]{1,0:T(8,128)(2,1)} %get-tuple-element.16), channel_id=1, source_target_pairs={{0,1},{1,0},{2,3},{3,2},{4,5},{5,4},{6,7},{7,6},{8,9},{9,8},{10,11... | collective-permute-start | bytes 1622024 | tf_op jit(solution)/shard_map/ppermute | solution.py:346
  9.6 15.7 %collective-permute-start.3 = (bf16[192,1408]{1,0:T(8,128)(2,1)S(1)}, bf16[192,1408]{1,0:T(8,128)(2,1)}, u32[]{:S(2)}, u32[]{:S(2)}) collective-permute-start(bf16[192,1408]{1,0:T(8,128)(2,1)S(1)} %get-tuple-element.15), channel_id=1, source_target_pairs={{0,2},{1,3},{2,0},{3,1},{4,6},{5,7},{6,4},{7,5},{8,10},{9,11},{10,... | collective-permute-start | bytes 1622024 | tf_op jit(solution)/shard_map/ppermute | solution.py:346
  12.1 24.4 %collective-permute-start.4 = (bf16[192,1408]{1,0:T(8,128)(2,1)S(1)}, bf16[192,1408]{1,0:T(8,128)(2,1)}, u32[]{:S(2)}, u32[]{:S(2)}) collective-permute-start(bf16[192,1408]{1,0:T(8,128)(2,1)S(1)} %get-tuple-element.14), channel_id=1, source_target_pairs={{0,3},{1,2},{2,1},{3,0},{4,7},{5,6},{6,5},{7,4},{8,11},{9,10},{10,... | collective-permute-start | bytes 1622024 | tf_op jit(solution)/shard_map/ppermute | solution.py:346
  27.2 14.3 %copy-start.9 = (bf16[384,2048]{1,0:T(8,128)(2,1)S(1)}, bf16[384,2048]{1,0:T(8,128)(2,1)}, u32[]{:S(2)}) copy-start(bf16[384,2048]{1,0:T(8,128)(2,1)} %param.20) | copy-start | bytes 4718596
  38.4 6.9 %copy-start.19 = (f32[16]{0:T(128)S(1)}, f32[16]{0:T(128)}, u32[]{:S(2)}) copy-start(f32[16]{0:T(128)} %param.29) | copy-start | bytes 196
  38.4 6.9 %copy-start.16 = (f32[2048]{0:T(1024)S(1)}, f32[2048]{0:T(1024)}, u32[]{:S(2)}) copy-start(f32[2048]{0:T(1024)} %param.22) | copy-start | bytes 24580
  41.5 5.6 %copy-start.14 = (bf16[2048,16]{0,1:T(8,128)(2,1)S(1)}, bf16[2048,16]{0,1:T(8,128)(2,1)}, u32[]{:S(2)}) copy-start(bf16[2048,16]{0,1:T(8,128)(2,1)} %param.28) | copy-start | bytes 196612
  41.5 5.6 %copy-start.15 = (bf16[2048,16]{0,1:T(8,128)(2,1)S(1)}, bf16[2048,16]{0,1:T(8,128)(2,1)}, u32[]{:S(2)}) copy-start(bf16[2048,16]{0,1:T(8,128)(2,1)} %param.27) | copy-start | bytes 196612
  41.5 199.7 %all-gather.8.cloned.1.call-start = ((), (), s32[]{:S(2)}) async-start(), calls=%async_computation.2 | async-start | bytes 6488064 | tf_op jit(solution)/shard_map/all_gather | solution.py:393
  42.2 5.4 %copy-start.18 = (f32[16]{0:T(128)S(1)}, f32[16]{0:T(128)}, u32[]{:S(2)}) copy-start(f32[16]{0:T(128)} %param.30) | copy-start | bytes 196
  42.2 5.9 %copy-start.20 = (s32[4]{0:T(128)S(1)}, s32[4]{0:T(128)}, u32[]{:S(2)}) copy-start(s32[4]{0:T(128)} %param.21) | copy-start | bytes 52
  42.2 20.9 %collective-permute-start = (bf16[16,2048]{1,0:T(8,128)(2,1)}, bf16[16,2048]{1,0:T(8,128)(2,1)}, u32[]{:S(2)}, u32[]{:S(2)}) collective-permute-start(bf16[16,2048]{1,0:T(8,128)(2,1)} %slice.60), channel_id=1, source_target_pairs={{0,1},{1,2},{2,3},{3,4},{4,5},{5,6},{6,7},{7,8},{8,9},{9,10},{10,1... | collective-permute-start | bytes 196616 | tf_op jit(solution)/shard_map/ppermute | solution.py:403
  49.8 287.1 %all-gather.6.cloned.1.call-start = ((), (), s32[]{:S(2)}) async-start(), calls=%async_computation.1 | async-start | bytes 6488064 | tf_op jit(solution)/shard_map/all_gather | solution.py:393
  50.1 15.1 %copy-start.12 = (bf16[384,2048]{1,0:T(8,128)(2,1)S(1)}, bf16[384,2048]{1,0:T(8,128)(2,1)}, u32[]{:S(2)}) copy-start(bf16[384,2048]{1,0:T(8,128)(2,1)} %copy-done.11) | copy-start | bytes 4718596
  62.9 9.4 %slice-start = ((s8[8388608]{0:T(1024)(128)(4,1)}), s8[4194304]{0:T(1024)(128)(4,1)S(1)}, s32[]{:S(2)}) async-start(s8[8388608]{0:T(1024)(128)(4,1)} %bitcast.80), calls=%async_computation.3 | async-start | bytes 8388608
  65.2 7.1 %slice-start.1 = ((s8[8388608]{0:T(1024)(128)(4,1)}), s8[4194304]{0:T(1024)(128)(4,1)S(1)}, s32[]{:S(2)}) async-start(s8[8388608]{0:T(1024)(128)(4,1)} %bitcast.80), calls=%async_computation.4 | async-start | bytes 8388608
  77.0 11.8 %copy-start.4 = (f32[4,4096]{1,0:T(4,128)S(1)}, f32[4,4096]{1,0:T(4,128)}, u32[]{:S(2)}) copy-start(f32[4,4096]{1,0:T(4,128)} %tv.1) | copy-start | bytes 196612
  77.0 11.8 %copy-start.5 = (f32[4,2048]{1,0:T(4,128)S(1)}, f32[4,2048]{1,0:T(4,128)}, u32[]{:S(2)}) copy-start(f32[4,2048]{1,0:T(4,128)} %tq.1) | copy-start | bytes 98308
  77.0 11.8 %copy-start.6 = (f32[4,2048]{1,0:T(4,128)S(1)}, f32[4,2048]{1,0:T(4,128)}, u32[]{:S(2)}) copy-start(f32[4,2048]{1,0:T(4,128)} %tk.1) | copy-start | bytes 98308
  147.3 17.0 %copy-start = (bf16[16,384,256]{2,1,0:T(8,128)(2,1)S(1)}, bf16[16,384,256]{2,1,0:T(8,128)(2,1)}, u32[]{:S(2)}) copy-start(bf16[16,384,256]{2,1,0:T(8,128)(2,1)} %get-tuple-element.9.oloc) | copy-start | bytes 9437188
  147.3 17.0 %copy-start.2 = (bf16[16,384,128]{2,1,0:T(8,128)(2,1)S(1)}, bf16[16,384,128]{2,1,0:T(8,128)(2,1)}, u32[]{:S(2)}) copy-start(bf16[16,384,128]{2,1,0:T(8,128)(2,1)} %copy-done.1) | copy-start | bytes 4718596
  147.3 17.0 %copy-start.3 = (f32[256]{0:T(256)S(1)}, f32[256]{0:T(256)}, u32[]{:S(2)}) copy-start(f32[256]{0:T(256)} %param.34) | copy-start | bytes 3076
  164.3 4.9 %copy-start.10 = (bf16[384,2048]{1,0:T(8,128)(2,1)S(1)}, bf16[384,2048]{1,0:T(8,128)(2,1)}, u32[]{:S(2)}) copy-start(bf16[384,2048]{1,0:T(8,128)(2,1)} %param.20) | copy-start | bytes 4718596
  169.2 10.6 %copy-start.17 = (f32[2048]{0:T(1024)S(1)}, f32[2048]{0:T(1024)}, u32[]{:S(2)}) copy-start(f32[2048]{0:T(1024)} %param.36) | copy-start | bytes 24580
  181.5 38.8 %collective-permute-start.6 = (bf16[384,2048]{1,0:T(8,128)(2,1)}, bf16[384,2048]{1,0:T(8,128)(2,1)S(1)}, u32[]{:S(2)}, u32[]{:S(2)}) collective-permute-start(bf16[384,2048]{1,0:T(8,128)(2,1)} %multiply_convert_fusion.2), channel_id=1, source_target_pairs={{0,2},{1,3},{2,0},{3,1},{4,6},{5,7},{6,4},{7,5},{8,10},{9,11},{10,... | collective-permute-start | bytes 4718600 | tf_op jit(solution)/shard_map/ppermute | solution.py:346
  220.3 5.6 %collective-permute-start.7 = (bf16[384,2048]{1,0:T(8,128)(2,1)S(1)}, bf16[384,2048]{1,0:T(8,128)(2,1)S(1)}, u32[]{:S(2)}, u32[]{:S(2)}) collective-permute-start(bf16[384,2048]{1,0:T(8,128)(2,1)S(1)} %collective-permute-done.6), channel_id=1, source_target_pairs={{0,1},{1,0},{2,3},{3,2},{4,5},{5,4},{6,7},{7,6},{8,9},{9,8},{10,11... | collective-permute-start | bytes 4718600 | tf_op jit(solution)/shard_map/ppermute | solution.py:346
  220.3 139.1 %collective-permute-start.1 = (bf16[384,2048]{1,0:T(8,128)(2,1)}, bf16[384,2048]{1,0:T(8,128)(2,1)}, u32[]{:S(2)}, u32[]{:S(2)}) collective-permute-start(bf16[384,2048]{1,0:T(8,128)(2,1)} %multiply_convert_fusion.2), channel_id=1, source_target_pairs={{0,1},{1,0},{2,3},{3,2},{4,5},{5,4},{6,7},{7,6},{8,9},{9,8},{10,11... | collective-permute-start | bytes 4718600 | tf_op jit(solution)/shard_map/ppermute | solution.py:346
  359.4 32.8 %collective-permute-start.8 = (bf16[384,2048]{1,0:T(8,128)(2,1)}, bf16[384,2048]{1,0:T(8,128)(2,1)}, u32[]{:S(2)}, u32[]{:S(2)}) collective-permute-start(bf16[384,2048]{1,0:T(8,128)(2,1)} %slice.138), channel_id=1, source_target_pairs={{0,1},{1,0},{2,3},{3,2},{4,5},{5,4},{6,7},{7,6},{8,9},{9,8},{10,11... | collective-permute-start | bytes 4718600 | tf_op jit(solution)/shard_map/ppermute | solution.py:346
  391.7 40.1 %copy-start.13 = (f32[768,2048]{1,0:T(8,128)S(1)}, f32[768,2048]{1,0:T(8,128)}, u32[]{:S(2)}) copy-start(f32[768,2048]{1,0:T(8,128)} %fusion.7) | copy-start | bytes 18874372
  391.7 5.3 %collective-permute-start.5 = (bf16[384,2048]{1,0:T(8,128)(2,1)S(1)}, bf16[384,2048]{1,0:T(8,128)(2,1)S(1)}, u32[]{:S(2)}, u32[]{:S(2)}) collective-permute-start(bf16[384,2048]{1,0:T(8,128)(2,1)S(1)} %slice.139), channel_id=1, source_target_pairs={{0,1},{1,0},{2,3},{3,2},{4,5},{5,4},{6,7},{7,6},{8,9},{9,8},{10,11... | collective-permute-start | bytes 4718600 | tf_op jit(solution)/shard_map/ppermute | solution.py:346
  395.4 36.3 %collective-permute-start.9 = (bf16[384,2048]{1,0:T(8,128)(2,1)S(1)}, bf16[384,2048]{1,0:T(8,128)(2,1)S(1)}, u32[]{:S(2)}, u32[]{:S(2)}) collective-permute-start(bf16[384,2048]{1,0:T(8,128)(2,1)S(1)} %fusion.3), channel_id=1, source_target_pairs={{0,2},{1,3},{2,0},{3,1},{4,6},{5,7},{6,4},{7,5},{8,10},{9,11},{10,... | collective-permute-start | bytes 4718600 | tf_op jit(solution)/shard_map/ppermute | solution.py:346
  (4 other events, 4.9 us)
Sparse Core Ops, SparseCore 0:
  41.6 94.1 all-gather.3
  138.0 103.1 all-gather.7
  243.4 93.5 all-gather.5

commit v3 on v2

--- a/solution.py
+++ b/solution.py
@@ -167,7 +167,7 @@
         ],
         compiler_params=pltpu.CompilerParams(vmem_limit_bytes=48 * 2**20),
         cost_estimate=pl.CostEstimate(
-            flops=heads * rows * 2000000, bytes_accessed=20 * 2**20, transcendentals=0
+            flops=10**9, bytes_accessed=20 * 2**20, transcendentals=0
         ),
         name="local_maps",
     )(pq, pk, pv, tq, tk, tv, scal)
@@ -217,12 +217,12 @@
 
     lax.fori_loop(0, per_core, join, 0)
 
-    def onward_copy(h):
+    def onward_copy(h, part):
         return pltpu.make_async_remote_copy(
-            src_ref=outgoing.at[h],
-            dst_ref=landing.at[h],
-            send_sem=send_sem.at[h],
-            recv_sem=recv_sem.at[h],
+            src_ref=outgoing.at[part, h],
+            dst_ref=landing.at[part, h],
+            send_sem=send_sem.at[part, h],
+            recv_sem=recv_sem.at[part, h],
             device_id={"req": me + 2},
             device_id_type=mesh_id,
         )
@@ -237,23 +237,28 @@
             device_id_type=mesh_id,
         )
 
+    parts = landing.shape[0]
+    width = landing.shape[3]
+
     def one(h, carry):
-        @pl.when(has_left)
-        def _():
-            onward_copy(h).wait_recv()
-
-        @pl.when(jnp.logical_not(has_left))
-        def _():
-            landing[h] = jnp.zeros(landing.shape[1:], BF16)
-
-        coming = landing[h]
-
-        @pl.when(has_right)
-        def _():
-            onward = mm(joined[h, :, :dk], coming) + joined[h, :, dk:].astype(F32)
-            outgoing[h] = onward.astype(BF16)
-            onward_copy(h).start()
-
+        for part in range(parts):
+            lanes = slice(dk + part * width, dk + (part + 1) * width)
+
+            @pl.when(has_left)
+            def _():
+                onward_copy(h, part).wait_recv()
+
+            @pl.when(jnp.logical_not(has_left))
+            def _():
+                landing[part, h] = jnp.zeros(landing.shape[2:], BF16)
+
+            @pl.when(has_right)
+            def _():
+                onward = mm(joined[h, :, :dk], landing[part, h])
+                outgoing[part, h] = (onward + joined[h, :, lanes].astype(F32)).astype(BF16)
+                onward_copy(h, part).start()
+
+        coming = jnp.concatenate([landing[part, h] for part in range(parts)], axis=1)
         middle = (mm(first[h, :, :dk], coming) + first[h, :, dk:].astype(F32)).astype(BF16)
         states[own_base + h] = jnp.where(core == 0, coming, middle)
         to_peer[h] = jnp.where(core == 0, middle, coming)
@@ -271,7 +276,8 @@
     lax.fori_loop(0, per_core, collect, 0)
 
     def drain(h, carry):
-        onward_copy(h).wait_send()
+        for part in range(parts):
+            onward_copy(h, part).wait_send()
         return carry
 
     @pl.when(has_right)
@@ -287,21 +293,26 @@
     per_core = heads // 2
     map_buf = pltpu.VMEM((per_core, dk, width), BF16)
     state_buf = pltpu.VMEM((per_core, dk, dv), BF16)
+    parts = dv // 128 if dv % 128 == 0 else 1
+    part_buf = pltpu.VMEM((parts, per_core, dk, dv // parts), BF16)
     sems = pltpu.SemaphoreType.DMA((per_core,))
+    part_sems = pltpu.SemaphoreType.DMA((parts, per_core))
     return pl.pallas_call(
         functools.partial(chain_kernel, n, dk),
         in_specs=[pl.BlockSpec(memory_space=pltpu.VMEM)],
         out_specs=pl.BlockSpec(memory_space=pltpu.VMEM),
         out_shape=jax.ShapeDtypeStruct((heads, dk, dv), BF16),
         scratch_shapes=[map_buf] * 3
-        + [state_buf] * 4
+        + [part_buf] * 2
+        + [state_buf] * 2
         + [pltpu.SemaphoreType.DMA] * 2
-        + [sems] * 4,
+        + [part_sems] * 2
+        + [sems] * 2,
         compiler_params=pltpu.CompilerParams(
             collective_id=0, has_side_effects=True, vmem_limit_bytes=32 * 2**20
         ),
         cost_estimate=pl.CostEstimate(
-            flops=60 * 10**9, bytes_accessed=3 * 2**20, transcendentals=0
+            flops=10**9, bytes_accessed=3 * 2**20, transcendentals=0
         ),
         name="chain_states",
     )(maps)
@@ -340,6 +351,10 @@
         ),
         name="finish_heads",
     )(qeff, oloc, states, gate, gain.reshape(1, dv))
+
+
+def zero_after(value):
+    return jnp.minimum(jnp.abs(value[0, 0].astype(F32)), 0.0).astype(jnp.int32)
 
 
 def swapped(value, n, bits):
@@ -377,35 +392,39 @@
     taps = conv_query.shape[0]
     chunk = 128
     count = rows // chunk
+    token_rows = gathered.astype(F32)
+    normed = rms_scale(token_rows, in_gain).astype(BF16)
+    gate_lin = mm(normed, w_gate).astype(BF16)
     group = 4
     spot = me % group
     quarter = w_up.shape[1] // group
     shards = jnp.concatenate([w_up_gate, w_up, w_down.T], axis=0)
     depth = w_up.shape[0]
     pieces = jnp.zeros((group,) + (shards.shape[0], quarter), BF16)
+    received = []
     for d in range(group):
         piece = lax.dynamic_slice_in_dim(shards, (spot ^ d) * quarter, quarter, 1)
-        if d:
-            piece = swapped(piece, n, d)
-        pieces = lax.dynamic_update_slice_in_dim(pieces, piece[None], spot ^ d, 0)
+        received.append(swapped(piece, n, d) if d else piece)
+    gated = zero_after(gate_lin)
+    for d in range(group):
+        place = (spot ^ d) + (gated if d else 0)
+        pieces = lax.dynamic_update_slice_in_dim(pieces, received[d][None], place, 0)
     members = [list(range(k, n, group)) for k in range(group)]
-    up_gate_part, up_part, down_part = [
-        lax.all_gather(
-            pieces[:, m * depth : (m + 1) * depth].reshape(group * depth, quarter),
-            "req",
-            axis=0,
-            tiled=True,
-            axis_index_groups=members,
-        )
+    blocks = [
+        pieces[:, m * depth : (m + 1) * depth].reshape(group * depth, quarter)
         for m in range(3)
     ]
-
+    mlp_part = lax.all_gather(
+        jnp.concatenate(blocks, axis=1),
+        "req",
+        axis=0,
+        tiled=True,
+        axis_index_groups=members,
+    )
     rim = lax.ppermute(gathered[rows - RIM :], "req", [(i, i + 1) for i in range(n - 1)])
-    token_rows = gathered.astype(F32)
-    normed = rms_scale(token_rows, in_gain).astype(BF16)
-    gate_lin = mm(normed, w_gate).astype(BF16)
     small = mm(normed, jnp.concatenate([w_beta, w_decay], axis=1))
-    rim_normed = rms_scale(rim.astype(F32), in_gain).astype(BF16)
+    rim = rim.astype(F32) + zero_after(pieces[0]).astype(F32)
+    rim_normed = rms_scale(rim, in_gain).astype(BF16)
     ext = jnp.concatenate([rim_normed, normed], axis=0)
     pq = mm(ext, w_query).astype(BF16)
     pk = mm(ext, w_key).astype(BF16)
@@ -454,19 +473,23 @@
         partial_out = lax.psum(partial_out.astype(BF16), "mlp").astype(F32)
     resid = token_rows + partial_out
     mlp_in = rms_scale(resid, mlp_gain).astype(BF16)
+    up_part, down_part = mlp_part[:, : 2 * quarter], mlp_part[:, 2 * quarter :]
     far_b = swapped(mlp_in, n, 2)
     near = jnp.concatenate([mlp_in, swapped(mlp_in, n, 1)], axis=0)
     far = jnp.concatenate([far_b, swapped(far_b, n, 1)], axis=0)
 
-    def hidden_of(x):
-        return (jax.nn.silu(mm(x, up_gate_part)) * mm(x, up_part)).astype(BF16)
-
-    near_hidden = hidden_of(near)
-    far_down = mm_t(hidden_of(far), down_part)
+    def swiglu(x):
+        acc = mm(x, up_part)
+        hidden = (jax.nn.silu(acc[:, :quarter]) * acc[:, quarter:]).astype(BF16)
+        return mm_t(hidden, down_part)
+
+    far_down = swiglu(far)
     far_chip = far_down[:rows] + swapped(far_down[rows:].astype(BF16), n, 1).astype(F32)
-    from_far = swapped(far_chip.astype(BF16), n, 2).astype(F32)
-    near_down = mm_t(near_hidden, down_part)
-    from_near = swapped(near_down[rows:].astype(BF16), n, 1).astype(F32)
+    far_chip = far_chip.astype(BF16)
+    from_far = swapped(far_chip, n, 2).astype(F32)
+    near_down = swiglu(near + zero_after(far_chip).astype(BF16))
+    near_send = near_down[rows:] + zero_after(from_far).astype(F32)
+    from_near = swapped(near_send.astype(BF16), n, 1).astype(F32)
     down = near_down[:rows] + from_near + from_far
     if lax.axis_size("mlp") > 1:
         down = lax.psum_scatter(

time: 444 us -> 464 us (1.045)
  waiting for transfers between devices: 190 us -> 232 us
  matrix products: 107 us -> 88.1 us
    all_gather x3 -> x1, waiting for transfers between devices: 99.7 us -> 172 us  [per_device(): lax.all_gather(jnp.concatenate(blocks, axis=1), 'req', axis=0, tiled=True...]
    ppermute x9, waiting for transfers between devices: 90.7 us -> 60.1 us  [swapped(): return lax.ppermute(value, 'req', [(i, i ^ bits) for i in range(n)])]
    dot_general x2, matrix products: 38.6 us -> 14.4 us  [mm_t(): lax.dot_general(a, b, (((1,), (1,)), ((), ())), preferred_element_type=F32)]
    dot_general x8, matrix products: 68.2 us -> 73.5 us  [mm(): return jnp.dot(a, b, preferred_element_type=F32)]
    ppermute x9, starting transfers between devices: 10.6 us -> 15.4 us  [swapped(): return lax.ppermute(value, 'req', [(i, i ^ bits) for i in range(n)])]
  transfers between devices with their start and end apart: 13 -> 11, of which waited for: 7 -> 8; matrix products, arithmetic and copies ran while one was open for 30% -> 18% of each run, Pallas kernels for 17% -> 17%
where the time goes in v3:
time: 464 us; the launch traced here: 463 us
  waiting for transfers between devices  232 us (50%)
  matrix products  88.1 us (19%)
  Pallas kernels  77.3 us (17%)
  local copies, waits for them, and re-layouts  22.3 us (5%)
  starting transfers between devices  17.5 us (4%)
  between operations  16.7 us (4%)
  other arithmetic  9.1 us (2%)
    all_gather x1, waiting for transfers between devices, per_device(): lax.all_gather(jnp.concatenate(blocks, axis=1), 'req', axis=0, tiled=True...  172 us
    dot_general x8, matrix products, mm(): return jnp.dot(a, b, preferred_element_type=F32)  73.5 us
    ppermute x9, waiting for transfers between devices, swapped(): return lax.ppermute(value, 'req', [(i, i ^ bits) for i in range(n)])  60.1 us
    pallas_call x1, Pallas kernels, local_maps(): pl.pallas_call(functools.partial(local_kernel, chunk, dk, dv), grid=(head...  54.6 us
    pallas_call x1, Pallas kernels, chain_states(): pl.pallas_call(functools.partial(chain_kernel, n, dk), in_specs=[pl.Block...  17.6 us
    ppermute x9, starting transfers between devices, swapped(): return lax.ppermute(value, 'req', [(i, i ^ bits) for i in range(n)])  15.4 us
    dot_general x2, matrix products, mm_t(): lax.dot_general(a, b, (((1,), (1,)), ((), ())), preferred_element_type=F32)  14.4 us
  transfers between devices with their start and end apart: 11, of which 8 were waited for; matrix products, arithmetic and copies ran while one was open for 18% of the time, Pallas kernels for 17%

profile of v3, /device:TPU:0, one launch (start us, length us, event | category | flops | bytes accessed | tf_op | source)
XLA Modules:
  0.0 462.9 jit_solution(4437628587427262713)
XLA Ops:
  6.5 1.8 pad_maximum_fusion
  10.1 2.5 collective-permute-start.2
  14.9 10.3 %convolution_convert_fusion.1.gate = bf16[384,4096]{1,0:T(8,128)(2,1)S(1)} fusion(bf16[384,2048]{1,0:T(8,128)(2,1)S(1)} %fusion.12, bf16[2048,4096]{1,0:T(8,128)(2,1)} %param.26), kind=kOutput, calls=%fused_computation.5 | convolution fusion | flops 6444023808 | bytes 21495808 | tf_op jit(solution)/shard_map/dot_general | solution.py:25
  25.3 1.5 broadcast_in_dim.30
  26.8 1.9 bitcast_dynamic-update-slice_fusion.3
  30.0 1.9 bitcast_dynamic-update-slice_fusion.2
  31.9 1.9 bitcast_dynamic-update-slice_fusion.1
  33.8 3.5 collective-permute-done.3
  37.3 1.9 bitcast_dynamic-update-slice_fusion
  39.2 1.7 fusion.62
  40.9 1.6 pad_maximum_fusion.1
  43.4 2.0 collective-permute-start
  45.4 2.0 fusion.28
  52.7 8.7 %convolution_convert_fusion.2.pk = bf16[400,2048]{1,0:T(8,128)(2,1)} fusion(bf16[2048,2048]{1,0:T(8,128)(2,1)} %param.24, bf16[384,2048]{1,0:T(8,128)(2,1)} %copy-done.8, bf16[16,2048]{1,0:T(8,128)(2,1)S(1)} %multiply_convert_fusion.1), kind=kOutput, calls=%fused_computation.37 | convolution fusion | flops 3359539200 | bytes 11665408 | tf_op jit(solution)/shard_map/dot_general | solution.py:25
  61.4 3.6 convolution_convert_fusion.3.pq
  65.1 12.0 %convolution_convert_fusion.pv = bf16[400,4096]{1,0:T(8,128)(2,1)} fusion(bf16[2048,4096]{1,0:T(8,128)(2,1)} %param.25, bf16[384,2048]{1,0:T(8,128)(2,1)S(1)} %copy-done.9, bf16[16,2048]{1,0:T(8,128)(2,1)S(1)} %multiply_convert_fusion.1), kind=kOutput, calls=%fused_computation.4 | convolution fusion | flops 6715801600 | bytes 21692416 | tf_op jit(solution)/shard_map/dot_general | solution.py:25
  77.1 54.6 %local_maps.1 = (bf16[16,384,128]{2,1,0:T(8,128)(2,1)S(1)}, bf16[16,384,256]{2,1,0:T(8,128)(2,1)}, bf16[16,128,384]{2,1,0:T(8,128)(2,1)S(1)}) custom-call(bf16[400,2048]{1,0:T(8,128)(2,1)S(1)} %convolution_convert_fusion.3.pq, bf16[400,2048]{1,0:T(8,128)(2,1)} %convolution_convert_fusion.2.pk, bf16[400,4096]{1,0:T(8,128)(2,1)} %convolution_convert_fusion.pv, ...), custom_call_target="tpu_custom_call" | custom-call | flops 1000000000 | bytes 20971520 | tf_op jit(solution)/shard_map/local_maps/pallas_call | solution.py:145
  131.7 17.6 %chain_states.1.states = bf16[16,128,256]{2,1,0:T(8,128)(2,1)S(1)} custom-call(bf16[16,128,384]{2,1,0:T(8,128)(2,1)S(1)} %get-tuple-element.10.maps), custom_call_target="tpu_custom_call" | custom-call | flops 1000000000 | bytes 3145728 | tf_op jit(solution)/shard_map/chain_states/pallas_call | solution.py:300
  149.3 5.1 %finish_heads.1 = bf16[384,4096]{1,0:T(8,128)(2,1)S(1)} custom-call(bf16[16,384,128]{2,1,0:T(8,128)(2,1)S(1)} %get-tuple-element.8.qeff, bf16[16,384,256]{2,1,0:T(8,128)(2,1)S(1)} %copy-done, bf16[16,128,256]{2,1,0:T(8,128)(2,1)S(1)} %chain_states.1.states, bf16[384,4096]{1,0:T(8,128)(2,1)S(1)} %convolution_convert_fusion.1.gate, f32[1,256]{1,0:T(1,128)S(1)} %bitcast.68), custom_call_target="tpu_custom_call" | custom-call | flops 402653184 | bytes 12582912 | tf_op jit(solution)/shard_map/finish_heads/pallas_call | solution.py:336
  154.5 10.4 %multiply_reduce_fusion = (f32[384]{0:T(512)S(1)}, f32[384,2048]{1,0:T(8,128)S(1)}) fusion(bf16[384,4096]{1,0:T(8,128)(2,1)S(1)} %finish_heads.1, bf16[4096,2048]{1,0:T(8,128)(2,1)} %param.35, bf16[384,2048]{1,0:T(8,128)(2,1)S(1)} %copy-done.7), kind=kOutput, calls=%fused_computation.36 | convolution fusion | flops 6445596160 | bytes 24643072 | tf_op jit(solution)/shard_map/dot_general | solution.py:25
  166.6 12.1 %collective-permute-start.5 = (bf16[384,2048]{1,0:T(8,128)(2,1)S(1)}, bf16[384,2048]{1,0:T(8,128)(2,1)S(1)}, u32[]{:S(2)}, u32[]{:S(2)}) collective-permute-start(bf16[384,2048]{1,0:T(8,128)(2,1)S(1)} %multiply_convert_fusion), channel_id=1, source_target_pairs={{0,2},{1,3},{2,0},{3,1},{4,6},{5,7},{6,4},{7,5},{8,10},{9,11},{10,... | collective-permute-start | bytes 4718600 | tf_op jit(solution)/shard_map/ppermute | solution.py:361
  178.7 31.7 %collective-permute-done.5 = bf16[384,2048]{1,0:T(8,128)(2,1)S(1)} collective-permute-done((bf16[384,2048]{1,0:T(8,128)(2,1)S(1)}, bf16[384,2048]{1,0:T(8,128)(2,1)S(1)}, u32[]{:S(2)}, u32[]{:S(2)}) %collective-permute-start.5) | collective-permute-done | bytes 1572896 | tf_op jit(solution)/shard_map/ppermute | solution.py:361
  211.5 3.5 collective-permute-done.6
  215.1 171.7 %all-gather.2.cloned.1.call-done = bf16[2048,4224]{1,0:T(8,128)(2,1)} async-done(((bf16[256,4224]{1,0:T(8,128)(2,1)}), bf16[2048,4224]{1,0:T(8,128)(2,1)}) %all-gather.2.cloned.1.call-update) | async-done | bytes 17301520 | tf_op jit(solution)/shard_map/all_gather | solution.py:417
  386.8 13.7 %fusion.2 = f32[768,2816]{1,0:T(8,128)S(1)} fusion(bf16[2048,4224]{1,0:T(8,128)(2,1)} %all-gather.2.cloned.1.call-done, bf16[384,2048]{1,0:T(8,128)(2,1)} %collective-permute-done.6, bf16[384,2048]{1,0:T(8,128)(2,1)} %copy-done.17), kind=kOutput, calls=%fused_computation.2 | convolution fusion | flops 8864661504 | bytes 23330816 | tf_op jit(solution)/shard_map/dot_general | solution.py:25
  400.4 7.2 %fusion.6 = f32[768,2048]{1,0:T(8,128)S(1)} fusion(bf16[2048,4224]{1,0:T(8,128)(2,1)} %all-gather.2.cloned.1.call-done, f32[768,2816]{1,0:T(8,128)S(1)} %fusion.2), kind=kOutput, calls=%fused_computation.8 | convolution fusion | flops 4435673088 | bytes 20709376 | tf_op jit(solution)/shard_map/dot_general | solution.py:29
  409.1 2.3 collective-permute-done.7
  413.6 12.8 %fusion = f32[768,2816]{1,0:T(8,128)S(1)} fusion(bf16[2048,4224]{1,0:T(8,128)(2,1)} %all-gather.2.cloned.1.call-done, bf16[384,2048]{1,0:T(8,128)(2,1)S(1)} %collective-permute-done.4, bf16[384,2048]{1,0:T(8,128)(2,1)S(1)} %copy-done.11, bf16[]{:T(256)} %bitcast.21), kind=kOutput, calls=%fused_computation | convolution fusion | flops 8867807232 | bytes 23331328 | tf_op jit(solution)/shard_map/dot_general | solution.py:25
  426.4 7.2 %fusion.4 = f32[768,2048]{1,0:T(8,128)S(1)} fusion(bf16[2048,4224]{1,0:T(8,128)(2,1)} %all-gather.2.cloned.1.call-done, f32[768,2816]{1,0:T(8,128)S(1)} %fusion), kind=kOutput, calls=%fused_computation.6 | convolution fusion | flops 4435673088 | bytes 20709376 | tf_op jit(solution)/shard_map/dot_general | solution.py:29
  433.6 15.2 %collective-permute-done.8 = bf16[384,2048]{1,0:T(8,128)(2,1)S(1)} collective-permute-done((bf16[384,2048]{1,0:T(8,128)(2,1)S(1)}, bf16[384,2048]{1,0:T(8,128)(2,1)S(1)}, u32[]{:S(2)}, u32[]{:S(2)}) %collective-permute-start.8) | collective-permute-done | bytes 1572896 | tf_op jit(solution)/shard_map/ppermute | solution.py:361
  450.4 3.4 collective-permute-done.9
  453.8 2.2 fusion.16
  (113 shorter events, 16.7 us)
Async XLA Ops:
  6.5 380.2 %all-gather.2.cloned.1.call-start = ((), (), s32[]{:S(2)}) async-start(), calls=%async_computation | async-start | bytes 19464192 | tf_op jit(solution)/shard_map/all_gather | solution.py:417
  6.5 6.2 %copy-start.6 = (bf16[384,2048]{1,0:T(8,128)(2,1)S(1)}, bf16[384,2048]{1,0:T(8,128)(2,1)}, u32[]{:S(2)}) copy-start(bf16[384,2048]{1,0:T(8,128)(2,1)} %param.20) | copy-start | bytes 4718596
  8.3 4.8 %copy-start.5 = (bf16[192,5632]{1,0:T(8,128)(2,1)}, bf16[192,5632]{1,0:T(8,128)(2,1)S(1)}, u32[]{:S(2)}) copy-start(bf16[192,5632]{1,0:T(8,128)(2,1)S(1)} %pad_maximum_fusion) | copy-start | bytes 6488068
  8.4 4.8 %copy-start.14 = (f32[2048]{0:T(1024)S(1)}, f32[2048]{0:T(1024)}, u32[]{:S(2)}) copy-start(f32[2048]{0:T(1024)} %param.22) | copy-start | bytes 24580
  9.7 20.3 %collective-permute-start.1 = (bf16[192,1408]{1,0:T(8,128)(2,1)}, bf16[192,1408]{1,0:T(8,128)(2,1)}, u32[]{:S(2)}, u32[]{:S(2)}) collective-permute-start(bf16[192,1408]{1,0:T(8,128)(2,1)} %get-tuple-element.16), channel_id=1, source_target_pairs={{0,1},{1,0},{2,3},{3,2},{4,5},{5,4},{6,7},{7,6},{8,9},{9,8},{10,11... | collective-permute-start | bytes 1622024 | tf_op jit(solution)/shard_map/ppermute | solution.py:361
  10.1 21.8 %collective-permute-start.2 = (bf16[192,1408]{1,0:T(8,128)(2,1)}, bf16[192,1408]{1,0:T(8,128)(2,1)}, u32[]{:S(2)}, u32[]{:S(2)}) collective-permute-start(bf16[192,1408]{1,0:T(8,128)(2,1)} %get-tuple-element.15), channel_id=1, source_target_pairs={{0,2},{1,3},{2,0},{3,1},{4,6},{5,7},{6,4},{7,5},{8,10},{9,11},{10,... | collective-permute-start | bytes 1622024 | tf_op jit(solution)/shard_map/ppermute | solution.py:361
  12.6 24.7 %collective-permute-start.3 = (bf16[192,1408]{1,0:T(8,128)(2,1)}, bf16[192,1408]{1,0:T(8,128)(2,1)}, u32[]{:S(2)}, u32[]{:S(2)}) collective-permute-start(bf16[192,1408]{1,0:T(8,128)(2,1)} %get-tuple-element.14), channel_id=1, source_target_pairs={{0,3},{1,2},{2,1},{3,0},{4,7},{5,6},{6,5},{7,4},{8,11},{9,10},{10,... | collective-permute-start | bytes 1622024 | tf_op jit(solution)/shard_map/ppermute | solution.py:361
  40.9 4.5 copy-start.18
  40.9 4.5 copy-start.12
  40.9 4.5 copy-start.13
  40.9 6.5 %copy-start.16 = (f32[16]{0:T(128)S(1)}, f32[16]{0:T(128)}, u32[]{:S(2)}) copy-start(f32[16]{0:T(128)} %param.30) | copy-start | bytes 196
  42.5 5.3 %copy-start.19 = (s32[4]{0:T(128)S(1)}, s32[4]{0:T(128)}, u32[]{:S(2)}) copy-start(s32[4]{0:T(128)} %param.21) | copy-start | bytes 52
  43.4 9.0 %collective-permute-start = (bf16[16,2048]{1,0:T(8,128)(2,1)S(1)}, bf16[16,2048]{1,0:T(8,128)(2,1)S(1)}, u32[]{:S(2)}, u32[]{:S(2)}) collective-permute-start(bf16[16,2048]{1,0:T(8,128)(2,1)S(1)} %slice.92), channel_id=1, source_target_pairs={{0,1},{1,2},{2,3},{3,4},{4,5},{5,6},{6,7},{7,8},{8,9},{9,10},{10,1... | collective-permute-start | bytes 196616 | tf_op jit(solution)/shard_map/ppermute | solution.py:424
  49.8 11.6 %slice-start = ((s8[8388608]{0:T(1024)(128)(4,1)}), s8[4194304]{0:T(1024)(128)(4,1)S(1)}, s32[]{:S(2)}) async-start(s8[8388608]{0:T(1024)(128)(4,1)} %bitcast.78), calls=%async_computation.1 | async-start | bytes 8388608
  52.6 8.8 %copy-start.9 = (bf16[384,2048]{1,0:T(8,128)(2,1)S(1)}, bf16[384,2048]{1,0:T(8,128)(2,1)}, u32[]{:S(2)}) copy-start(bf16[384,2048]{1,0:T(8,128)(2,1)} %copy-done.8) | copy-start | bytes 4718596
  52.6 8.8 %slice-start.1 = ((s8[8388608]{0:T(1024)(128)(4,1)}), s8[4194304]{0:T(1024)(128)(4,1)S(1)}, s32[]{:S(2)}) async-start(s8[8388608]{0:T(1024)(128)(4,1)} %bitcast.78), calls=%async_computation.2 | async-start | bytes 8388608
  65.1 12.1 %copy-start.1 = (f32[4,4096]{1,0:T(4,128)S(1)}, f32[4,4096]{1,0:T(4,128)}, u32[]{:S(2)}) copy-start(f32[4,4096]{1,0:T(4,128)} %tv.1) | copy-start | bytes 196612
  65.1 12.0 %copy-start.2 = (f32[4,2048]{1,0:T(4,128)S(1)}, f32[4,2048]{1,0:T(4,128)}, u32[]{:S(2)}) copy-start(f32[4,2048]{1,0:T(4,128)} %tq.1) | copy-start | bytes 98308
  65.1 12.0 %copy-start.3 = (f32[4,2048]{1,0:T(4,128)S(1)}, f32[4,2048]{1,0:T(4,128)}, u32[]{:S(2)}) copy-start(f32[4,2048]{1,0:T(4,128)} %tk.1) | copy-start | bytes 98308
  131.7 17.6 %copy-start = (bf16[16,384,256]{2,1,0:T(8,128)(2,1)S(1)}, bf16[16,384,256]{2,1,0:T(8,128)(2,1)}, u32[]{:S(2)}) copy-start(bf16[16,384,256]{2,1,0:T(8,128)(2,1)} %get-tuple-element.9.oloc) | copy-start | bytes 9437188
  131.7 17.6 %copy-start.4 = (f32[256]{0:T(256)S(1)}, f32[256]{0:T(256)}, u32[]{:S(2)}) copy-start(f32[256]{0:T(256)} %param.34) | copy-start | bytes 3076
  149.3 5.2 %copy-start.7 = (bf16[384,2048]{1,0:T(8,128)(2,1)S(1)}, bf16[384,2048]{1,0:T(8,128)(2,1)}, u32[]{:S(2)}) copy-start(bf16[384,2048]{1,0:T(8,128)(2,1)} %param.20) | copy-start | bytes 4718596
  154.5 10.4 %copy-start.15 = (f32[2048]{0:T(1024)S(1)}, f32[2048]{0:T(1024)}, u32[]{:S(2)}) copy-start(f32[2048]{0:T(1024)} %param.36) | copy-start | bytes 24580
  165.4 1.1 copy-start.10
  166.6 43.8 %collective-permute-start.5 = (bf16[384,2048]{1,0:T(8,128)(2,1)S(1)}, bf16[384,2048]{1,0:T(8,128)(2,1)S(1)}, u32[]{:S(2)}, u32[]{:S(2)}) collective-permute-start(bf16[384,2048]{1,0:T(8,128)(2,1)S(1)} %multiply_convert_fusion), channel_id=1, source_target_pairs={{0,2},{1,3},{2,0},{3,1},{4,6},{5,7},{6,4},{7,5},{8,10},{9,11},{10,... | collective-permute-start | bytes 4718600 | tf_op jit(solution)/shard_map/ppermute | solution.py:361
  210.3 1.2 copy-start.17
  211.5 3.5 collective-permute-start.6
  407.6 1.4 copy-start.11
  407.9 3.5 collective-permute-start.7
  409.1 4.6 collective-permute-start.4
  412.4 36.4 %collective-permute-start.8 = (bf16[384,2048]{1,0:T(8,128)(2,1)S(1)}, bf16[384,2048]{1,0:T(8,128)(2,1)S(1)}, u32[]{:S(2)}, u32[]{:S(2)}) collective-permute-start(bf16[384,2048]{1,0:T(8,128)(2,1)S(1)} %fusion.17), channel_id=1, source_target_pairs={{0,2},{1,3},{2,0},{3,1},{4,6},{5,7},{6,4},{7,5},{8,10},{9,11},{10,... | collective-permute-start | bytes 4718600 | tf_op jit(solution)/shard_map/ppermute | solution.py:361
  450.3 3.5 collective-permute-start.9
  (1 other events, 1.1 us)
Sparse Core Ops, SparseCore 0:
  42.6 344.0 all-gather.1

commit v4 on v3

--- a/solution.py
+++ b/solution.py
@@ -414,13 +414,11 @@
         pieces[:, m * depth : (m + 1) * depth].reshape(group * depth, quarter)
         for m in range(3)
     ]
-    mlp_part = lax.all_gather(
-        jnp.concatenate(blocks, axis=1),
-        "req",
-        axis=0,
-        tiled=True,
-        axis_index_groups=members,
-    )
+    up_part, down_part = [
+        lax.all_gather(block, "req", axis=0, tiled=True, axis_index_groups=members)
+        for block in (jnp.concatenate(blocks[:2], axis=1), blocks[2])
+    ]
+
     rim = lax.ppermute(gathered[rows - RIM :], "req", [(i, i + 1) for i in range(n - 1)])
     small = mm(normed, jnp.concatenate([w_beta, w_decay], axis=1))
     rim = rim.astype(F32) + zero_after(pieces[0]).astype(F32)
@@ -473,7 +471,6 @@
         partial_out = lax.psum(partial_out.astype(BF16), "mlp").astype(F32)
     resid = token_rows + partial_out
     mlp_in = rms_scale(resid, mlp_gain).astype(BF16)
-    up_part, down_part = mlp_part[:, : 2 * quarter], mlp_part[:, 2 * quarter :]
     far_b = swapped(mlp_in, n, 2)
     near = jnp.concatenate([mlp_in, swapped(mlp_in, n, 1)], axis=0)
     far = jnp.concatenate([far_b, swapped(far_b, n, 1)], axis=0)

time: 464 us -> 377 us (0.81)
  waiting for transfers between devices: 232 us -> 140 us
  matrix products: 88.1 us -> 95.5 us
  starting transfers between devices: 17.5 us -> 11.6 us
    all_gather x1 -> x2, waiting for transfers between devices: 172 us -> 81.3 us  [per_device(): lax.all_gather(block, 'req', axis=0, tiled=True, axis_index_groups=members)]
    ppermute x9, starting transfers between devices: 15.4 us -> 8.83 us  [swapped(): return lax.ppermute(value, 'req', [(i, i ^ bits) for i in range(n)])]
  transfers between devices with their start and end apart: 11 -> 12, of which waited for: 8 -> 8; matrix products, arithmetic and copies ran while one was open for 18% -> 28% of each run, Pallas kernels for 17% -> 20%
where the time goes in v4:
time: 377 us; the launch traced here: 376 us
  waiting for transfers between devices  140 us (37%)
  matrix products  95.5 us (25%)
  Pallas kernels  76.6 us (20%)
  local copies, waits for them, and re-layouts  25.1 us (7%)
  between operations  16.8 us (4%)
  starting transfers between devices  11.6 us (3%)
  other arithmetic  10.6 us (3%)
    all_gather x2, waiting for transfers between devices, per_device(): lax.all_gather(block, 'req', axis=0, tiled=True, axis_index_groups=members)  81.3 us
    dot_general x8, matrix products, mm(): return jnp.dot(a, b, preferred_element_type=F32)  76.7 us
    ppermute x9, waiting for transfers between devices, swapped(): return lax.ppermute(value, 'req', [(i, i ^ bits) for i in range(n)])  58.7 us
    pallas_call x1, Pallas kernels, local_maps(): pl.pallas_call(functools.partial(local_kernel, chunk, dk, dv), grid=(head...  54.5 us
    dot_general x2, matrix products, mm_t(): lax.dot_general(a, b, (((1,), (1,)), ((), ())), preferred_element_type=F32)  18.6 us
    pallas_call x1, Pallas kernels, chain_states(): pl.pallas_call(functools.partial(chain_kernel, n, dk), in_specs=[pl.Block...  17 us
    ppermute x9, starting transfers between devices, swapped(): return lax.ppermute(value, 'req', [(i, i ^ bits) for i in range(n)])  8.83 us
    dynamic_update_slice x4, local copies, waits for them, and re-layouts, per_device(): lax.dynamic_update_slice_in_dim(pieces, received[d][None], place, 0)  7.63 us
  transfers between devices with their start and end apart: 12, of which 8 were waited for; matrix products, arithmetic and copies ran while one was open for 28% of the time, Pallas kernels for 20%

profile of v4, /device:TPU:0, one launch (start us, length us, event | category | flops | bytes accessed | tf_op | source)
XLA Modules:
  0.0 376.3 jit_solution(9990356935502005659)
XLA Ops:
  6.5 1.8 pad_maximum_fusion
  10.1 2.5 collective-permute-start.2
  14.9 10.3 %convolution_convert_fusion.1.gate = bf16[384,4096]{1,0:T(8,128)(2,1)S(1)} fusion(bf16[384,2048]{1,0:T(8,128)(2,1)S(1)} %fusion.4, bf16[2048,4096]{1,0:T(8,128)(2,1)} %param.26), kind=kOutput, calls=%fused_computation.1 | convolution fusion | flops 6444023808 | bytes 21495808 | tf_op jit(solution)/shard_map/dot_general | solution.py:25
  25.2 1.6 broadcast_in_dim.30
  26.8 1.9 bitcast_dynamic-update-slice_fusion.3
  30.0 1.9 bitcast_dynamic-update-slice_fusion.2
  31.9 2.0 bitcast_dynamic-update-slice_fusion.1
  33.9 3.4 collective-permute-done.3
  37.3 1.9 bitcast_dynamic-update-slice_fusion
  39.2 2.6 fusion.58
  44.5 2.7 collective-permute-start
  47.3 2.0 fusion.24
  56.3 8.7 %convolution_convert_fusion.2.pk = bf16[400,2048]{1,0:T(8,128)(2,1)} fusion(bf16[2048,2048]{1,0:T(8,128)(2,1)} %param.24, bf16[384,2048]{1,0:T(8,128)(2,1)} %copy-done.9, bf16[16,2048]{1,0:T(8,128)(2,1)S(1)} %multiply_convert_fusion.1), kind=kOutput, calls=%fused_computation.31 | convolution fusion | flops 3359539200 | bytes 11665408 | tf_op jit(solution)/shard_map/dot_general | solution.py:25
  65.1 4.8 %convolution_convert_fusion.3.pq = bf16[400,2048]{1,0:T(8,128)(2,1)} fusion(bf16[2048,2048]{1,0:T(8,128)(2,1)S(1)} %bitcast.83, bf16[384,2048]{1,0:T(8,128)(2,1)S(1)} %copy-done.10, bf16[16,2048]{1,0:T(8,128)(2,1)S(1)} %multiply_convert_fusion.1), kind=kOutput, calls=%fused_computation.32 | convolution fusion | flops 3359539200 | bytes 11665408 | tf_op jit(solution)/shard_map/dot_general | solution.py:25
  70.0 12.3 %convolution_convert_fusion.pv = bf16[400,4096]{1,0:T(8,128)(2,1)} fusion(bf16[2048,4096]{1,0:T(8,128)(2,1)} %param.25, bf16[384,2048]{1,0:T(8,128)(2,1)} %copy-done.9, bf16[16,2048]{1,0:T(8,128)(2,1)} %copy-done.13), kind=kOutput, calls=%fused_computation | convolution fusion | flops 6715801600 | bytes 21692416 | tf_op jit(solution)/shard_map/dot_general | solution.py:25
  82.2 54.5 %local_maps.1 = (bf16[16,384,128]{2,1,0:T(8,128)(2,1)S(1)}, bf16[16,384,256]{2,1,0:T(8,128)(2,1)}, bf16[16,128,384]{2,1,0:T(8,128)(2,1)S(1)}) custom-call(bf16[400,2048]{1,0:T(8,128)(2,1)S(1)} %copy-done.1, bf16[400,2048]{1,0:T(8,128)(2,1)} %convolution_convert_fusion.2.pk, bf16[400,4096]{1,0:T(8,128)(2,1)} %convolution_convert_fusion.pv, ...), custom_call_target="tpu_custom_call" | custom-call | flops 1000000000 | bytes 20971520 | tf_op jit(solution)/shard_map/local_maps/pallas_call | solution.py:145
  136.8 17.0 %chain_states.1.states = bf16[16,128,256]{2,1,0:T(8,128)(2,1)S(1)} custom-call(bf16[16,128,384]{2,1,0:T(8,128)(2,1)S(1)} %get-tuple-element.10.maps), custom_call_target="tpu_custom_call" | custom-call | flops 1000000000 | bytes 3145728 | tf_op jit(solution)/shard_map/chain_states/pallas_call | solution.py:300
  153.8 5.1 %finish_heads.1 = bf16[384,4096]{1,0:T(8,128)(2,1)S(1)} custom-call(bf16[16,384,128]{2,1,0:T(8,128)(2,1)S(1)} %get-tuple-element.8.qeff, bf16[16,384,256]{2,1,0:T(8,128)(2,1)S(1)} %copy-done, bf16[16,128,256]{2,1,0:T(8,128)(2,1)S(1)} %chain_states.1.states, bf16[384,4096]{1,0:T(8,128)(2,1)S(1)} %convolution_convert_fusion.1.gate, f32[1,256]{1,0:T(1,128)S(1)} %bitcast.72), custom_call_target="tpu_custom_call" | custom-call | flops 402653184 | bytes 12582912 | tf_op jit(solution)/shard_map/finish_heads/pallas_call | solution.py:336
  159.0 10.6 %multiply_reduce_fusion = (f32[384]{0:T(512)S(1)}, f32[384,2048]{1,0:T(8,128)S(1)}) fusion(bf16[384,4096]{1,0:T(8,128)(2,1)S(1)} %finish_heads.1, bf16[4096,2048]{1,0:T(8,128)(2,1)} %param.35, bf16[384,2048]{1,0:T(8,128)(2,1)S(1)} %copy-done.8), kind=kOutput, calls=%fused_computation.30 | convolution fusion | flops 6445596160 | bytes 24643072 | tf_op jit(solution)/shard_map/dot_general | solution.py:25
  171.3 4.1 %collective-permute-start.5 = (bf16[384,2048]{1,0:T(8,128)(2,1)S(1)}, bf16[384,2048]{1,0:T(8,128)(2,1)S(1)}, u32[]{:S(2)}, u32[]{:S(2)}) collective-permute-start(bf16[384,2048]{1,0:T(8,128)(2,1)S(1)} %multiply_convert_fusion), channel_id=1, source_target_pairs={{0,2},{1,3},{2,0},{3,1},{4,6},{5,7},{6,4},{7,5},{8,10},{9,11},{10,... | collective-permute-start | bytes 4718600 | tf_op jit(solution)/shard_map/ppermute | solution.py:361
  175.4 34.4 %collective-permute-done.5 = bf16[384,2048]{1,0:T(8,128)(2,1)S(1)} collective-permute-done((bf16[384,2048]{1,0:T(8,128)(2,1)S(1)}, bf16[384,2048]{1,0:T(8,128)(2,1)S(1)}, u32[]{:S(2)}, u32[]{:S(2)}) %collective-permute-start.5) | collective-permute-done | bytes 1572896 | tf_op jit(solution)/shard_map/ppermute | solution.py:361
  211.0 3.5 collective-permute-done.6
  215.4 15.7 %fusion.13 = f32[768,2816]{1,0:T(8,128)} fusion(bf16[2048,2816]{1,0:T(8,128)(2,1)} %all-gather.3.cloned.1.call-done, bf16[384,2048]{1,0:T(8,128)(2,1)} %collective-permute-done.6, bf16[384,2048]{1,0:T(8,128)(2,1)} %copy-done.21), kind=kOutput, calls=%fused_computation.25 | convolution fusion | flops 8864661504 | bytes 23330816 | tf_op jit(solution)/shard_map/dot_general | solution.py:25
  231.2 80.4 %all-gather.5.cloned.1.call-done = bf16[2048,1408]{1,0:T(8,128)(2,1)} async-done(((bf16[256,1408]{1,0:T(8,128)(2,1)}), bf16[2048,1408]{1,0:T(8,128)(2,1)}) %all-gather.5.cloned.1.call-update) | async-done | bytes 5767184 | tf_op jit(solution)/shard_map/all_gather | solution.py:418
  311.6 9.4 %fusion.17 = f32[768,2048]{1,0:T(8,128)S(1)} fusion(bf16[2048,1408]{1,0:T(8,128)(2,1)} %all-gather.5.cloned.1.call-done, f32[768,2816]{1,0:T(8,128)} %fusion.13), kind=kOutput, calls=%fused_computation.33 | convolution fusion | flops 4435673088 | bytes 20709376 | tf_op jit(solution)/shard_map/dot_general | solution.py:29
  322.4 2.3 collective-permute-done.7
  325.7 1.5 collective-permute-start.8
  329.0 12.2 %fusion.10 = f32[768,2816]{1,0:T(8,128)} fusion(bf16[2048,2816]{1,0:T(8,128)(2,1)S(1)} %copy-done.19, bf16[384,2048]{1,0:T(8,128)(2,1)} %copy-done.20, bf16[384,2048]{1,0:T(8,128)(2,1)S(1)} %copy-done.12, bf16[]{:T(256)} %bitcast.21), kind=kOutput, calls=%fused_computation.22 | convolution fusion | flops 8867807232 | bytes 23330818 | tf_op jit(solution)/shard_map/dot_general | solution.py:25
  341.3 9.3 %fusion.19 = f32[768,2048]{1,0:T(8,128)S(1)} fusion(bf16[2048,1408]{1,0:T(8,128)(2,1)} %all-gather.5.cloned.1.call-done, f32[768,2816]{1,0:T(8,128)} %fusion.10), kind=kOutput, calls=%fused_computation.34 | convolution fusion | flops 4435673088 | bytes 20709376 | tf_op jit(solution)/shard_map/dot_general | solution.py:29
  350.5 11.7 %collective-permute-done.8 = bf16[384,2048]{1,0:T(8,128)(2,1)S(1)} collective-permute-done((bf16[384,2048]{1,0:T(8,128)(2,1)S(1)}, bf16[384,2048]{1,0:T(8,128)(2,1)S(1)}, u32[]{:S(2)}, u32[]{:S(2)}) %collective-permute-start.8) | collective-permute-done | bytes 1572896 | tf_op jit(solution)/shard_map/ppermute | solution.py:361
  363.7 3.4 collective-permute-done.9
  367.1 2.3 fusion.8
  (124 shorter events, 21.7 us)
Async XLA Ops:
  6.5 208.9 %all-gather.3.cloned.1.call-start = ((), (), s32[]{:S(2)}) async-start(), calls=%async_computation | async-start | bytes 12976128 | tf_op jit(solution)/shard_map/all_gather | solution.py:418
  6.5 6.2 %copy-start.7 = (bf16[384,2048]{1,0:T(8,128)(2,1)S(1)}, bf16[384,2048]{1,0:T(8,128)(2,1)}, u32[]{:S(2)}) copy-start(bf16[384,2048]{1,0:T(8,128)(2,1)} %param.20) | copy-start | bytes 4718596
  8.3 4.8 %copy-start.6 = (bf16[192,5632]{1,0:T(8,128)(2,1)}, bf16[192,5632]{1,0:T(8,128)(2,1)S(1)}, u32[]{:S(2)}) copy-start(bf16[192,5632]{1,0:T(8,128)(2,1)S(1)} %pad_maximum_fusion) | copy-start | bytes 6488068
  9.7 20.4 %collective-permute-start.1 = (bf16[192,1408]{1,0:T(8,128)(2,1)}, bf16[192,1408]{1,0:T(8,128)(2,1)}, u32[]{:S(2)}, u32[]{:S(2)}) collective-permute-start(bf16[192,1408]{1,0:T(8,128)(2,1)} %get-tuple-element.16), channel_id=1, source_target_pairs={{0,1},{1,0},{2,3},{3,2},{4,5},{5,4},{6,7},{7,6},{8,9},{9,8},{10,11... | collective-permute-start | bytes 1622024 | tf_op jit(solution)/shard_map/ppermute | solution.py:361
  10.1 21.8 %collective-permute-start.2 = (bf16[192,1408]{1,0:T(8,128)(2,1)}, bf16[192,1408]{1,0:T(8,128)(2,1)}, u32[]{:S(2)}, u32[]{:S(2)}) collective-permute-start(bf16[192,1408]{1,0:T(8,128)(2,1)} %get-tuple-element.15), channel_id=1, source_target_pairs={{0,2},{1,3},{2,0},{3,1},{4,6},{5,7},{6,4},{7,5},{8,10},{9,11},{10,... | collective-permute-start | bytes 1622024 | tf_op jit(solution)/shard_map/ppermute | solution.py:361
  12.6 24.7 %collective-permute-start.3 = (bf16[192,1408]{1,0:T(8,128)(2,1)}, bf16[192,1408]{1,0:T(8,128)(2,1)}, u32[]{:S(2)}, u32[]{:S(2)}) collective-permute-start(bf16[192,1408]{1,0:T(8,128)(2,1)} %get-tuple-element.14), channel_id=1, source_target_pairs={{0,3},{1,2},{2,1},{3,0},{4,7},{5,6},{6,5},{7,4},{8,11},{9,10},{10,... | collective-permute-start | bytes 1622024 | tf_op jit(solution)/shard_map/ppermute | solution.py:361
  41.7 5.5 %copy-start.22 = (f32[16]{0:T(128)S(1)}, f32[16]{0:T(128)}, u32[]{:S(2)}) copy-start(f32[16]{0:T(128)} %param.29) | copy-start | bytes 196
  41.7 5.5 %copy-start.14 = (bf16[2048,16]{0,1:T(8,128)(2,1)S(1)}, bf16[2048,16]{0,1:T(8,128)(2,1)}, u32[]{:S(2)}) copy-start(bf16[2048,16]{0,1:T(8,128)(2,1)} %param.28) | copy-start | bytes 196612
  41.7 5.5 %copy-start.15 = (bf16[2048,16]{0,1:T(8,128)(2,1)S(1)}, bf16[2048,16]{0,1:T(8,128)(2,1)}, u32[]{:S(2)}) copy-start(bf16[2048,16]{0,1:T(8,128)(2,1)} %param.27) | copy-start | bytes 196612
  41.7 7.5 %copy-start.18 = (f32[16]{0:T(128)S(1)}, f32[16]{0:T(128)}, u32[]{:S(2)}) copy-start(f32[16]{0:T(128)} %param.30) | copy-start | bytes 196
  41.7 7.9 %copy-start.23 = (s32[4]{0:T(128)S(1)}, s32[4]{0:T(128)}, u32[]{:S(2)}) copy-start(s32[4]{0:T(128)} %param.21) | copy-start | bytes 52
  43.0 268.6 %all-gather.5.cloned.1.call-start = ((), (), s32[]{:S(2)}) async-start(), calls=%async_computation.1 | async-start | bytes 6488064 | tf_op jit(solution)/shard_map/all_gather | solution.py:418
  44.5 9.8 %collective-permute-start = (bf16[16,2048]{1,0:T(8,128)(2,1)}, bf16[16,2048]{1,0:T(8,128)(2,1)}, u32[]{:S(2)}, u32[]{:S(2)}) collective-permute-start(bf16[16,2048]{1,0:T(8,128)(2,1)} %slice.86), channel_id=1, source_target_pairs={{0,1},{1,2},{2,3},{3,4},{4,5},{5,6},{6,7},{7,8},{8,9},{9,10},{10,1... | collective-permute-start | bytes 196616 | tf_op jit(solution)/shard_map/ppermute | solution.py:422
  51.6 13.4 %slice-start = ((s8[8388608]{0:T(1024)(128)(4,1)}), s8[4194304]{0:T(1024)(128)(4,1)S(1)}, s32[]{:S(2)}) async-start(s8[8388608]{0:T(1024)(128)(4,1)} %bitcast.82), calls=%async_computation.2 | async-start | bytes 8388608
  56.3 8.8 %copy-start.13 = (bf16[16,2048]{1,0:T(8,128)(2,1)}, bf16[16,2048]{1,0:T(8,128)(2,1)S(1)}, u32[]{:S(2)}) copy-start(bf16[16,2048]{1,0:T(8,128)(2,1)S(1)} %multiply_convert_fusion.1) | copy-start | bytes 196612
  56.3 8.8 %copy-start.10 = (bf16[384,2048]{1,0:T(8,128)(2,1)S(1)}, bf16[384,2048]{1,0:T(8,128)(2,1)}, u32[]{:S(2)}) copy-start(bf16[384,2048]{1,0:T(8,128)(2,1)} %copy-done.9) | copy-start | bytes 4718596
  56.3 8.7 %slice-start.1 = ((s8[8388608]{0:T(1024)(128)(4,1)}), s8[4194304]{0:T(1024)(128)(4,1)S(1)}, s32[]{:S(2)}) async-start(s8[8388608]{0:T(1024)(128)(4,1)} %bitcast.82), calls=%async_computation.3 | async-start | bytes 8388608
  69.9 12.3 %copy-start.1 = (bf16[400,2048]{1,0:T(8,128)(2,1)S(1)}, bf16[400,2048]{1,0:T(8,128)(2,1)}, u32[]{:S(2)}) copy-start(bf16[400,2048]{1,0:T(8,128)(2,1)} %convolution_convert_fusion.3.pq) | copy-start | bytes 4915204
  69.9 12.3 %copy-start.2 = (f32[4,4096]{1,0:T(4,128)S(1)}, f32[4,4096]{1,0:T(4,128)}, u32[]{:S(2)}) copy-start(f32[4,4096]{1,0:T(4,128)} %tv.1) | copy-start | bytes 196612
  69.9 12.3 %copy-start.3 = (f32[4,2048]{1,0:T(4,128)S(1)}, f32[4,2048]{1,0:T(4,128)}, u32[]{:S(2)}) copy-start(f32[4,2048]{1,0:T(4,128)} %tq.1) | copy-start | bytes 98308
  70.0 12.3 %copy-start.4 = (f32[4,2048]{1,0:T(4,128)S(1)}, f32[4,2048]{1,0:T(4,128)}, u32[]{:S(2)}) copy-start(f32[4,2048]{1,0:T(4,128)} %tk.1) | copy-start | bytes 98308
  136.8 17.0 %copy-start = (bf16[16,384,256]{2,1,0:T(8,128)(2,1)S(1)}, bf16[16,384,256]{2,1,0:T(8,128)(2,1)}, u32[]{:S(2)}) copy-start(bf16[16,384,256]{2,1,0:T(8,128)(2,1)} %get-tuple-element.9.oloc) | copy-start | bytes 9437188
  136.8 17.0 %copy-start.5 = (f32[256]{0:T(256)S(1)}, f32[256]{0:T(256)}, u32[]{:S(2)}) copy-start(f32[256]{0:T(256)} %param.34) | copy-start | bytes 3076
  153.8 5.1 %copy-start.8 = (bf16[384,2048]{1,0:T(8,128)(2,1)S(1)}, bf16[384,2048]{1,0:T(8,128)(2,1)}, u32[]{:S(2)}) copy-start(bf16[384,2048]{1,0:T(8,128)(2,1)} %param.20) | copy-start | bytes 4718596
  158.9 10.7 %copy-start.17 = (f32[2048]{0:T(1024)S(1)}, f32[2048]{0:T(1024)}, u32[]{:S(2)}) copy-start(f32[2048]{0:T(1024)} %param.36) | copy-start | bytes 24580
  171.3 38.6 %collective-permute-start.5 = (bf16[384,2048]{1,0:T(8,128)(2,1)S(1)}, bf16[384,2048]{1,0:T(8,128)(2,1)S(1)}, u32[]{:S(2)}, u32[]{:S(2)}) collective-permute-start(bf16[384,2048]{1,0:T(8,128)(2,1)S(1)} %multiply_convert_fusion), channel_id=1, source_target_pairs={{0,2},{1,3},{2,0},{3,1},{4,6},{5,7},{6,4},{7,5},{8,10},{9,11},{10,... | collective-permute-start | bytes 4718600 | tf_op jit(solution)/shard_map/ppermute | solution.py:361
  211.0 3.5 collective-permute-start.6
  311.6 17.5 %copy-start.19 = (bf16[2048,2816]{1,0:T(8,128)(2,1)S(1)}, bf16[2048,2816]{1,0:T(8,128)(2,1)}, u32[]{:S(2)}) copy-start(bf16[2048,2816]{1,0:T(8,128)(2,1)} %all-gather.3.cloned.1.call-done) | copy-start | bytes 34603012
  321.2 3.5 collective-permute-start.7
  322.4 5.5 %collective-permute-start.4 = (bf16[384,2048]{1,0:T(8,128)(2,1)S(1)}, bf16[384,2048]{1,0:T(8,128)(2,1)S(1)}, u32[]{:S(2)}, u32[]{:S(2)}) collective-permute-start(bf16[384,2048]{1,0:T(8,128)(2,1)S(1)} %copy-done.12), channel_id=1, source_target_pairs={{0,1},{1,0},{2,3},{3,2},{4,5},{5,4},{6,7},{7,6},{8,9},{9,8},{10,11... | collective-permute-start | bytes 4718600 | tf_op jit(solution)/shard_map/ppermute | solution.py:361
  325.7 36.4 %collective-permute-start.8 = (bf16[384,2048]{1,0:T(8,128)(2,1)S(1)}, bf16[384,2048]{1,0:T(8,128)(2,1)S(1)}, u32[]{:S(2)}, u32[]{:S(2)}) collective-permute-start(bf16[384,2048]{1,0:T(8,128)(2,1)S(1)} %fusion.9), channel_id=1, source_target_pairs={{0,2},{1,3},{2,0},{3,1},{4,6},{5,7},{6,4},{7,5},{8,10},{9,11},{10,... | collective-permute-start | bytes 4718600 | tf_op jit(solution)/shard_map/ppermute | solution.py:361
  363.7 3.5 collective-permute-start.9
  (6 other events, 10.8 us)
Sparse Core Ops, SparseCore 0:
  43.1 172.2 all-gather.2
  217.6 93.8 all-gather.4
